TPU v7x, 32 devices: a whole 2x2x4 slice. The times are simulated.
32 devices in a mesh: member: 2 (over y), gridy: 4 (over x, core), gridx: 4 (over z).
Axes of the slice: x: 2, y: 2, z: 4, core: 2. Of those that a mesh axis runs over, the one named last changes fastest.
Arguments:
- temp: float32 [4, 4, 256, 1024], P('member', None, 'gridy', 'gridx'), may hold values from -6 to 6
- salt: float32 [4, 4, 256, 1024], P('member', None, 'gridy', 'gridx'), may hold values from -6 to 6
- uvel: float32 [4, 4, 256, 1024], P('member', None, 'gridy', 'gridx'), may hold values from -3 to 3
- vvel: float32 [4, 4, 256, 1024], P('member', None, 'gridy', 'gridx'), may hold values from -3 to 3
- eta: float32 [4, 256, 1024], P('member', 'gridy', 'gridx'), may hold values from -6 to 6
- land_mask: int32 [256, 1024], P('gridy', 'gridx'), may hold values 0 or 1
- clone_source: int32 [4], P('member'), may hold values from 0 to 3
Outputs:
- new_temp: float32 [4, 4, 256, 1024], P('member', None, 'gridy', 'gridx')
- new_salt: float32 [4, 4, 256, 1024], P('member', None, 'gridy', 'gridx')
- new_uvel: float32 [4, 4, 256, 1024], P('member', None, 'gridy', 'gridx')
- new_vvel: float32 [4, 4, 256, 1024], P('member', None, 'gridy', 'gridx')
- new_eta: float32 [4, 256, 1024], P('member', 'gridy', 'gridx')
- overturning: float32 [4, 4, 256], P('member', None, 'gridy')
- clone_weight: float32 [4], P('member')
All inputs are finite; a program needn't handle non-finite values. No bound on the sum of `land_mask` on one device may be relied on, other than what follows from the above.
Results may differ from a plain program's by a relative error of at most 0.0001.
Values sent between devices are 32-bit elements; how exact they have to be, the bound alone decides.
No kernel may reach another device: no remote copies, remote signals or barrier semaphores. Data moves between devices by JAX's collectives and lax.ppermute only.
A program may use at most 128 MiB of HBM per device.

v0:
```python
import jax
import jax.numpy as jnp
from jax import lax
from jax.sharding import PartitionSpec as P

STEPS = 2
ITERS = 3


ALPHA_T = 0.8
BETA_S = 0.6
PRESS_K = 0.25
STEP_DT = 0.1
KAPPA = 0.1
VISCOSITY = 0.1
DRAG_K = 0.05
CORI_K = 1.0
SURF_C = 4.0
DIV_K = 0.5
GRAV_K = 0.5


def padded_2(block, sides, width):
    for axis, dim in sides:
        count = lax.axis_size(axis)
        forward = [(i, i + 1) for i in range(count - 1)]
        forward.append((count - 1, 0))
        backward = [(target, source) for source, target in forward]
        low = lax.ppermute(
            lax.slice_in_dim(block, block.shape[dim] - width, None, axis=dim), axis, forward
        )
        high = lax.ppermute(lax.slice_in_dim(block, 0, width, axis=dim), axis, backward)
        block = jnp.concatenate([low, block, high], axis=dim)
    return block


def pressure(temp, salt):
    return PRESS_K * jnp.cumsum(BETA_S * salt - ALPHA_T * temp, axis=-3)


def split_rims(padded, south_keep, north_keep):
    east_side = padded[..., 1:-1, 2:]
    west_side = padded[..., 1:-1, :-2]
    north_side = padded[..., 2:, 1:-1]
    south_side = padded[..., :-2, 1:-1]
    north_side = north_side.at[..., -1, :].multiply(north_keep)
    south_side = south_side.at[..., 0, :].multiply(south_keep)
    return (east_side, west_side, north_side, south_side)


def volume_sides(fields, south_keep, north_keep):
    padded = padded_2(jnp.stack(fields), (("gridy", 3), ("gridx", 4)), 1)
    return split_rims(padded, south_keep, north_keep)


def surface_sides(fields, south_keep, north_keep):
    padded = padded_2(jnp.stack(fields), (("gridy", 2), ("gridx", 3)), 1)
    return split_rims(padded, south_keep, north_keep)


def surface_apply(field, south_keep, north_keep):
    east_side, west_side, north_side, south_side = surface_sides((field,), south_keep, north_keep)
    return (1.0 + 4.0 * SURF_C) * field - SURF_C * (
        east_side[0] + west_side[0] + north_side[0] + south_side[0]
    )


def member_total(values):
    return jnp.sum(values, axis=(1, 2))


def squared_norm(residual):
    return lax.psum(member_total(residual * residual), ("gridy", "gridx"))


def widen(values):
    return values[:, None, None]


def surface_solve(rhs, south_keep, north_keep):
    solution = jnp.zeros_like(rhs)
    residual = rhs
    direction = rhs
    norm_now = squared_norm(residual)
    for count in range(ITERS):
        image = surface_apply(direction, south_keep, north_keep)
        alpha = norm_now / lax.psum(member_total(direction * image), ("gridy", "gridx"))
        solution = solution + widen(alpha) * direction
        residual = residual - widen(alpha) * image
        norm_next = squared_norm(residual)
        direction = residual + widen(norm_next / norm_now) * direction
        norm_now = norm_next
    return solution


def shards(temp, salt, uvel, vvel, eta, land_mask, clone_source):
    levels = temp.shape[1]
    rows = temp.shape[2]
    cols = temp.shape[3]
    ocean = land_mask.astype(jnp.float32)
    tile_row = lax.axis_index("gridy")
    tile_count = lax.axis_size("gridy")
    total_rows = rows * tile_count
    total_cols = cols * lax.axis_size("gridx")
    south_keep = (tile_row > 0).astype(jnp.float32)
    north_keep = (tile_row < tile_count - 1).astype(jnp.float32)
    latitude = (tile_row * rows + jnp.arange(rows, dtype=jnp.int32)).astype(jnp.float32) + 0.5
    coriolis = (CORI_K * (2.0 * latitude / total_rows - 1.0))[:, None]
    for count in range(STEPS):
        press = pressure(temp, salt)
        east_side, west_side, north_side, south_side = volume_sides(
            (temp, salt, uvel, vvel, press), south_keep, north_keep
        )
        lap_temp = east_side[0] + west_side[0] + north_side[0] + south_side[0] - 4.0 * temp
        lap_salt = east_side[1] + west_side[1] + north_side[1] + south_side[1] - 4.0 * salt
        lap_uvel = east_side[2] + west_side[2] + north_side[2] + south_side[2] - 4.0 * uvel
        lap_vvel = east_side[3] + west_side[3] + north_side[3] + south_side[3] - 4.0 * vvel
        temp_next = ocean * (
            temp
            - STEP_DT
            * 0.5
            * (uvel * (east_side[0] - west_side[0]) + vvel * (north_side[0] - south_side[0]))
            + KAPPA * lap_temp
        )
        salt_next = ocean * (
            salt
            - STEP_DT
            * 0.5
            * (uvel * (east_side[1] - west_side[1]) + vvel * (north_side[1] - south_side[1]))
            + KAPPA * lap_salt
        )
        ustar = ocean * (
            uvel
            + STEP_DT * (coriolis * vvel - 0.5 * (east_side[4] - west_side[4]) - DRAG_K * uvel)
            + VISCOSITY * lap_uvel
        )
        vstar = ocean * (
            vvel
            + STEP_DT * (-coriolis * uvel - 0.5 * (north_side[4] - south_side[4]) - DRAG_K * vvel)
            + VISCOSITY * lap_vvel
        )
        trans_u = jnp.sum(ustar, axis=1)
        trans_v = jnp.sum(vstar, axis=1)
        east_t, west_t, north_t, south_t = surface_sides((trans_u, trans_v), south_keep, north_keep)
        rhs = eta - DIV_K * 0.5 * (east_t[0] - west_t[0] + (north_t[1] - south_t[1]))
        eta = surface_solve(rhs, south_keep, north_keep)
        east_e, west_e, north_e, south_e = surface_sides((eta,), south_keep, north_keep)
        uvel = ocean * (ustar - GRAV_K * 0.5 * (east_e[0] - west_e[0])[:, None])
        vvel = ocean * (vstar - GRAV_K * 0.5 * (north_e[0] - south_e[0])[:, None])
        temp = temp_next
        salt = salt_next
    zonal_scale = 1.0 / jnp.sqrt(jnp.float32(total_cols))
    score_scale = 1.0 / jnp.sqrt(jnp.float32(levels * total_rows))
    lat_weight = latitude / total_rows
    zonal_local = jnp.sum(vvel, axis=3)
    zonal_whole = lax.psum(zonal_local, "gridx")
    overturn = jnp.cumsum(zonal_whole, axis=1) * zonal_scale
    score = lax.psum(jnp.sum(overturn * lat_weight, axis=(1, 2)) * score_scale, "gridy")
    state_stack = jnp.stack((temp, salt, uvel, vvel))
    every_state, every_eta, every_score = (
        lax.all_gather(state_stack, "member", axis=1, tiled=True),
        lax.all_gather(eta, "member", axis=0, tiled=True),
        lax.all_gather(score, "member", axis=0, tiled=True),
    )
    picked = jnp.take(every_state, clone_source, axis=1)
    new_eta = jnp.take(every_eta, clone_source, axis=0)
    clone_weight = jnp.take(every_score, clone_source, axis=0) - jnp.mean(every_score)
    return (picked[0], picked[1], picked[2], picked[3], new_eta, overturn, clone_weight)


def solution(mesh):
    in_specs = (
        P("member", None, "gridy", "gridx"),
        P("member", None, "gridy", "gridx"),
        P("member", None, "gridy", "gridx"),
        P("member", None, "gridy", "gridx"),
        P("member", "gridy", "gridx"),
        P("gridy", "gridx"),
        P("member"),
    )
    out_specs = (
        P("member", None, "gridy", "gridx"),
        P("member", None, "gridy", "gridx"),
        P("member", None, "gridy", "gridx"),
        P("member", None, "gridy", "gridx"),
        P("member", "gridy", "gridx"),
        P("member", None, "gridy"),
        P("member"),
    )
    return jax.shard_map(shards, mesh=mesh, in_specs=in_specs, out_specs=out_specs, check_vma=False)
```

profile of v0, /device:TPU:0, one launch (start us, length us, event | category | flops | bytes accessed | tf_op | source)
XLA Modules:
  0.0 617.0 jit_solution(1765588832480175306)
XLA Ops:
  47.5 3.8 collective-permute-start.6
  51.5 4.4 collective-permute-done.7
  66.7 31.5 %all-reduce.2 = (f32[2]{0:T(128)S(1)}, f32[2]{0:T(128)S(1)}) all-reduce(f32[2]{0:T(128)S(1)} %get-tuple-element.298, f32[2]{0:T(128)S(1)} %get-tuple-element.297), channel_id=1, replica_groups=mesh['member'=2,'gridy'=4,'gridx'=4] {'gridy','gridx'}, use_global_device_ids=true, to_apply=%region_4.5 | all-reduce | flops 4 | bytes 32 | tf_op jit(solution)/shard_map/psum | solution.py:73
  98.4 30.1 %psum.100 = f32[2]{0:T(128)S(1)} all-reduce(f32[2]{0:T(128)S(1)} %get-tuple-element.316), channel_id=1, replica_groups=mesh['member'=2,'gridy'=4,'gridx'=4] {'gridy','gridx'}, use_global_device_ids=true, to_apply=%region_8.9 | all-reduce | flops 2 | bytes 16 | tf_op jit(solution)/shard_map/psum | solution.py:73
  139.1 31.4 %psum.101 = f32[2]{0:T(128)S(1)} all-reduce(f32[2]{0:T(128)S(1)} %get-tuple-element.314), channel_id=1, replica_groups=mesh['member'=2,'gridy'=4,'gridx'=4] {'gridy','gridx'}, use_global_device_ids=true, to_apply=%region_10.11 | all-reduce | flops 2 | bytes 16 | tf_op jit(solution)/shard_map/psum | solution.py:87
  170.7 30.2 %psum.102 = f32[2]{0:T(128)S(1)} all-reduce(f32[2]{0:T(128)S(1)} %multiply_reduce_fusion.5), channel_id=1, replica_groups=mesh['member'=2,'gridy'=4,'gridx'=4] {'gridy','gridx'}, use_global_device_ids=true, to_apply=%region_12.13 | all-reduce | flops 2 | bytes 16 | tf_op jit(solution)/shard_map/psum | solution.py:73
  212.5 3.5 bitcast_dynamic-update-slice_fusion.3
  216.0 32.0 %psum.103 = f32[2]{0:T(128)} all-reduce(f32[2]{0:T(128)} %fusion.143), channel_id=1, replica_groups=mesh['member'=2,'gridy'=4,'gridx'=4] {'gridy','gridx'}, use_global_device_ids=true, to_apply=%region_14.15 | all-reduce | flops 2 | bytes 16 | tf_op jit(solution)/shard_map/psum | solution.py:87
  251.4 3.5 bitcast_dynamic-update-slice_fusion.2
  278.0 3.8 collective-permute-start.26
  295.4 3.4 fusion.175
  305.9 3.8 collective-permute-start.30
  330.1 30.3 %all-reduce.1 = (f32[2]{0:T(128)}, f32[2]{0:T(128)}) all-reduce(f32[2]{0:T(128)} %get-tuple-element.296, f32[2]{0:T(128)} %get-tuple-element.295), channel_id=1, replica_groups=mesh['member'=2,'gridy'=4,'gridx'=4] {'gridy','gridx'}, use_global_device_ids=true, to_apply=%region_19.20 | all-reduce | flops 4 | bytes 32 | tf_op jit(solution)/shard_map/psum | solution.py:73
  362.4 32.0 %psum.106 = f32[2]{0:T(128)S(1)} all-reduce(f32[2]{0:T(128)} %get-tuple-element.307), channel_id=1, replica_groups=mesh['member'=2,'gridy'=4,'gridx'=4] {'gridy','gridx'}, use_global_device_ids=true, to_apply=%region_23.24 | all-reduce | flops 2 | bytes 16 | tf_op jit(solution)/shard_map/psum | solution.py:73
  400.0 3.8 collective-permute-start.38
  410.7 30.3 %psum.107 = f32[2]{0:T(128)} all-reduce(f32[2]{0:T(128)} %get-tuple-element.305), channel_id=1, replica_groups=mesh['member'=2,'gridy'=4,'gridx'=4] {'gridy','gridx'}, use_global_device_ids=true, to_apply=%region_25.26 | all-reduce | flops 2 | bytes 16 | tf_op jit(solution)/shard_map/psum | solution.py:87
  444.0 32.5 %psum.108 = f32[2]{0:T(128)} all-reduce(f32[2]{0:T(128)} %multiply_reduce_fusion), channel_id=1, replica_groups=mesh['member'=2,'gridy'=4,'gridx'=4] {'gridy','gridx'}, use_global_device_ids=true, to_apply=%region_27.28 | all-reduce | flops 2 | bytes 16 | tf_op jit(solution)/shard_map/psum | solution.py:73
  482.2 3.8 collective-permute-start.42
  492.5 30.3 %psum.109 = f32[2]{0:T(128)} all-reduce(f32[2]{0:T(128)} %fusion.107), channel_id=1, replica_groups=mesh['member'=2,'gridy'=4,'gridx'=4] {'gridy','gridx'}, use_global_device_ids=true, to_apply=%region_29.30 | all-reduce | flops 2 | bytes 16 | tf_op jit(solution)/shard_map/psum | solution.py:87
  547.0 11.3 %psum.110 = f32[2,4,64]{2,1,0:T(4,128)S(1)} all-reduce(f32[2,4,64]{2,1,0:T(4,128)S(1)} %copy-done.41), channel_id=1, replica_groups=mesh['member'=2,'gridy'=4,'gridx'=4] {'gridx'}, use_global_device_ids=true, to_apply=%region_31.32 | all-reduce | flops 512 | bytes 4096 | tf_op jit(solution)/shard_map/psum | solution.py:156
  558.9 8.4 %all_gather.10 = f32[4,64,256]{2,1,0:T(8,128)S(1)} all-gather(f32[2,64,256]{2,1,0:T(8,128)S(1)} %copy-done.28), channel_id=1, replica_groups=mesh['member'=2,'gridy'=4,'gridx'=4] {'member'}, dimensions={0}, use_global_device_ids=true | all-gather | bytes 393216 | tf_op jit(solution)/shard_map/all_gather | solution.py:162
  567.3 6.0 psum.111
  574.2 5.0 all-reduce
  582.3 23.3 %all-gather.2.cloned.1.call-done = f32[4,4,4,64,256]{4,3,2,1,0:T(8,128)} async-done(((f32[4,2,4,64,256]{4,3,2,1,0:T(8,128)}), f32[4,4,4,64,256]{4,3,2,1,0:T(8,128)}) %all-gather.2.cloned.1.call-update) | async-done | bytes 4194320 | tf_op jit(solution)/shard_map/all_gather | solution.py:161
  (365 shorter events, 202.2 us)
Async XLA Ops:
  7.2 598.5 %all-gather.2.cloned.1.call-start = ((), (), s32[]{:S(2)}) async-start(), calls=%async_computation | async-start | bytes 6291456 | tf_op jit(solution)/shard_map/all_gather | solution.py:161
  21.3 13.3 %collective-permute-start.3 = (f32[5,2,4,66,1]{3,2,4,1,0:T(4,128)S(1)}, f32[5,2,4,66,1]{3,2,4,1,0:T(4,128)S(1)}, u32[]{:S(2)}, u32[]{:S(2)}) collective-permute-start(f32[5,2,4,66,1]{3,2,4,1,0:T(4,128)S(1)} %copy.16), channel_id=1, source_target_pairs={{0,1},{1,2},{2,3},{3,0},{4,5},{5,6},{6,7},{7,4},{8,9},{9,10},{10,1... | collective-permute-start | bytes 31688 | tf_op jit(solution)/shard_map/ppermute | solution.py:29
  24.8 11.5 %collective-permute-start.2 = (f32[5,2,4,66,1]{3,2,4,1,0:T(4,128)S(1)}, f32[5,2,4,66,1]{3,2,4,1,0:T(4,128)S(1)}, u32[]{:S(2)}, u32[]{:S(2)}) collective-permute-start(f32[5,2,4,66,1]{3,2,4,1,0:T(4,128)S(1)} %copy.14), channel_id=1, source_target_pairs={{1,0},{2,1},{3,2},{0,3},{5,4},{6,5},{7,6},{4,7},{9,8},{10,9},{11,1... | collective-permute-start | bytes 31688 | tf_op jit(solution)/shard_map/ppermute | solution.py:32
  47.4 8.4 %collective-permute-start.7 = (f32[2,2,66,1]{3,2,1,0:T(8,128)S(1)}, f32[2,2,66,1]{3,2,1,0:T(8,128)S(1)}, u32[]{:S(2)}, u32[]{:S(2)}) collective-permute-start(f32[2,2,66,1]{3,2,1,0:T(8,128)S(1)} %get-tuple-element.348), channel_id=1, source_target_pairs={{0,1},{1,2},{2,3},{3,0},{4,5},{5,6},{6,7},{7,4},{8,9},{9,10},{10,1... | collective-permute-start | bytes 3176 | tf_op jit(solution)/shard_map/ppermute | solution.py:29
  47.5 8.4 %collective-permute-start.6 = (f32[2,2,66,1]{3,2,1,0:T(8,128)S(1)}, f32[2,2,66,1]{3,2,1,0:T(8,128)S(1)}, u32[]{:S(2)}, u32[]{:S(2)}) collective-permute-start(f32[2,2,66,1]{3,2,1,0:T(8,128)S(1)} %get-tuple-element.347), channel_id=1, source_target_pairs={{1,0},{2,1},{3,2},{0,3},{5,4},{6,5},{7,6},{4,7},{9,8},{10,9},{11,1... | collective-permute-start | bytes 3176 | tf_op jit(solution)/shard_map/ppermute | solution.py:32
  60.2 6.2 %collective-permute-start.11 = (f32[1,2,66,1]{3,2,1,0:T(8,128)S(1)}, f32[1,2,66,1]{3,2,1,0:T(8,128)S(1)}, u32[]{:S(2)}, u32[]{:S(2)}) collective-permute-start(f32[1,2,66,1]{3,2,1,0:T(8,128)S(1)} %get-tuple-element.372), channel_id=1, source_target_pairs={{0,1},{1,2},{2,3},{3,0},{4,5},{5,6},{6,7},{7,4},{8,9},{9,10},{10,1... | collective-permute-start | bytes 1592 | tf_op jit(solution)/shard_map/ppermute | solution.py:29
  61.1 5.4 collective-permute-start.10
  131.8 6.4 %collective-permute-start.15 = (f32[1,2,66,1]{3,2,1,0:T(8,128)S(1)}, f32[1,2,66,1]{3,2,1,0:T(8,128)S(1)}, u32[]{:S(2)}, u32[]{:S(2)}) collective-permute-start(f32[1,2,66,1]{3,2,1,0:T(8,128)S(1)} %get-tuple-element.370), channel_id=1, source_target_pairs={{0,1},{1,2},{2,3},{3,0},{4,5},{5,6},{6,7},{7,4},{8,9},{9,10},{10,1... | collective-permute-start | bytes 1592 | tf_op jit(solution)/shard_map/ppermute | solution.py:29
  204.7 6.4 %collective-permute-start.19 = (f32[1,2,66,1]{3,2,1,0:T(8,128)S(1)}, f32[1,2,66,1]{3,2,1,0:T(8,128)S(1)}, u32[]{:S(2)}, u32[]{:S(2)}) collective-permute-start(f32[1,2,66,1]{3,2,1,0:T(8,128)S(1)} %get-tuple-element.368), channel_id=1, source_target_pairs={{0,1},{1,2},{2,3},{3,0},{4,5},{5,6},{6,7},{7,4},{8,9},{9,10},{10,1... | collective-permute-start | bytes 1592 | tf_op jit(solution)/shard_map/ppermute | solution.py:29
  249.7 5.3 collective-permute-start.20
  249.7 5.2 collective-permute-start.21
  255.1 6.4 %collective-permute-start.23 = (f32[1,2,66,1]{3,2,1,0:T(8,128)S(1)}, f32[1,2,66,1]{3,2,1,0:T(8,128)S(1)}, u32[]{:S(2)}, u32[]{:S(2)}) collective-permute-start(f32[1,2,66,1]{3,2,1,0:T(8,128)S(1)} %get-tuple-element.366), channel_id=1, source_target_pairs={{0,1},{1,2},{2,3},{3,0},{4,5},{5,6},{6,7},{7,4},{8,9},{9,10},{10,1... | collective-permute-start | bytes 1592 | tf_op jit(solution)/shard_map/ppermute | solution.py:29
  255.8 5.7 collective-permute-start.22
  275.5 15.0 %collective-permute-start.27 = (f32[5,2,4,66,1]{3,2,4,1,0:T(4,128)}, f32[5,2,4,66,1]{3,2,4,1,0:T(4,128)}, u32[]{:S(2)}, u32[]{:S(2)}) collective-permute-start(f32[5,2,4,66,1]{3,2,4,1,0:T(4,128)} %copy.20), channel_id=1, source_target_pairs={{0,1},{1,2},{2,3},{3,0},{4,5},{5,6},{6,7},{7,4},{8,9},{9,10},{10,1... | collective-permute-start | bytes 31688 | tf_op jit(solution)/shard_map/ppermute | solution.py:29
  278.0 14.9 %collective-permute-start.26 = (f32[5,2,4,66,1]{3,2,4,1,0:T(4,128)}, f32[5,2,4,66,1]{3,2,4,1,0:T(4,128)}, u32[]{:S(2)}, u32[]{:S(2)}) collective-permute-start(f32[5,2,4,66,1]{3,2,4,1,0:T(4,128)} %copy.18), channel_id=1, source_target_pairs={{1,0},{2,1},{3,2},{0,3},{5,4},{6,5},{7,6},{4,7},{9,8},{10,9},{11,1... | collective-permute-start | bytes 31688 | tf_op jit(solution)/shard_map/ppermute | solution.py:32
  305.9 8.8 %collective-permute-start.31 = (f32[2,2,66,1]{3,2,1,0:T(8,128)}, f32[2,2,66,1]{3,2,1,0:T(8,128)}, u32[]{:S(2)}, u32[]{:S(2)}) collective-permute-start(f32[2,2,66,1]{3,2,1,0:T(8,128)} %get-tuple-element.346), channel_id=1, source_target_pairs={{0,1},{1,2},{2,3},{3,0},{4,5},{5,6},{6,7},{7,4},{8,9},{9,10},{10,1... | collective-permute-start | bytes 3176 | tf_op jit(solution)/shard_map/ppermute | solution.py:29
  305.9 8.8 %collective-permute-start.30 = (f32[2,2,66,1]{3,2,1,0:T(8,128)}, f32[2,2,66,1]{3,2,1,0:T(8,128)}, u32[]{:S(2)}, u32[]{:S(2)}) collective-permute-start(f32[2,2,66,1]{3,2,1,0:T(8,128)} %get-tuple-element.345), channel_id=1, source_target_pairs={{1,0},{2,1},{3,2},{0,3},{5,4},{6,5},{7,6},{4,7},{9,8},{10,9},{11,1... | collective-permute-start | bytes 3176 | tf_op jit(solution)/shard_map/ppermute | solution.py:32
  319.9 7.7 %collective-permute-start.35 = (f32[1,2,66,1]{3,2,1,0:T(8,128)}, f32[1,2,66,1]{3,2,1,0:T(8,128)}, u32[]{:S(2)}, u32[]{:S(2)}) collective-permute-start(f32[1,2,66,1]{3,2,1,0:T(8,128)} %get-tuple-element.364), channel_id=1, source_target_pairs={{0,1},{1,2},{2,3},{3,0},{4,5},{5,6},{6,7},{7,4},{8,9},{9,10},{10,1... | collective-permute-start | bytes 1592 | tf_op jit(solution)/shard_map/ppermute | solution.py:29
  320.7 7.6 %collective-permute-start.34 = (f32[1,2,66,1]{3,2,1,0:T(8,128)}, f32[1,2,66,1]{3,2,1,0:T(8,128)}, u32[]{:S(2)}, u32[]{:S(2)}) collective-permute-start(f32[1,2,66,1]{3,2,1,0:T(8,128)} %get-tuple-element.363), channel_id=1, source_target_pairs={{1,0},{2,1},{3,2},{0,3},{5,4},{6,5},{7,6},{4,7},{9,8},{10,9},{11,1... | collective-permute-start | bytes 1592 | tf_op jit(solution)/shard_map/ppermute | solution.py:32
  400.0 8.4 %collective-permute-start.39 = (f32[1,2,66,1]{3,2,1,0:T(8,128)}, f32[1,2,66,1]{3,2,1,0:T(8,128)}, u32[]{:S(2)}, u32[]{:S(2)}) collective-permute-start(f32[1,2,66,1]{3,2,1,0:T(8,128)} %get-tuple-element.362), channel_id=1, source_target_pairs={{0,1},{1,2},{2,3},{3,0},{4,5},{5,6},{6,7},{7,4},{8,9},{9,10},{10,1... | collective-permute-start | bytes 1592 | tf_op jit(solution)/shard_map/ppermute | solution.py:29
  400.0 8.3 %collective-permute-start.38 = (f32[1,2,66,1]{3,2,1,0:T(8,128)}, f32[1,2,66,1]{3,2,1,0:T(8,128)}, u32[]{:S(2)}, u32[]{:S(2)}) collective-permute-start(f32[1,2,66,1]{3,2,1,0:T(8,128)} %get-tuple-element.361), channel_id=1, source_target_pairs={{1,0},{2,1},{3,2},{0,3},{5,4},{6,5},{7,6},{4,7},{9,8},{10,9},{11,1... | collective-permute-start | bytes 1592 | tf_op jit(solution)/shard_map/ppermute | solution.py:32
  482.1 8.4 %collective-permute-start.43 = (f32[1,2,66,1]{3,2,1,0:T(8,128)}, f32[1,2,66,1]{3,2,1,0:T(8,128)}, u32[]{:S(2)}, u32[]{:S(2)}) collective-permute-start(f32[1,2,66,1]{3,2,1,0:T(8,128)} %get-tuple-element.360), channel_id=1, source_target_pairs={{0,1},{1,2},{2,3},{3,0},{4,5},{5,6},{6,7},{7,4},{8,9},{9,10},{10,1... | collective-permute-start | bytes 1592 | tf_op jit(solution)/shard_map/ppermute | solution.py:29
  482.2 8.4 %collective-permute-start.42 = (f32[1,2,66,1]{3,2,1,0:T(8,128)}, f32[1,2,66,1]{3,2,1,0:T(8,128)}, u32[]{:S(2)}, u32[]{:S(2)}) collective-permute-start(f32[1,2,66,1]{3,2,1,0:T(8,128)} %get-tuple-element.359), channel_id=1, source_target_pairs={{1,0},{2,1},{3,2},{0,3},{5,4},{6,5},{7,6},{4,7},{9,8},{10,9},{11,1... | collective-permute-start | bytes 1592 | tf_op jit(solution)/shard_map/ppermute | solution.py:32
  527.8 6.4 %collective-permute-start.47 = (f32[1,2,66,1]{3,2,1,0:T(8,128)S(1)}, f32[1,2,66,1]{3,2,1,0:T(8,128)S(1)}, u32[]{:S(2)}, u32[]{:S(2)}) collective-permute-start(f32[1,2,66,1]{3,2,1,0:T(8,128)S(1)} %get-tuple-element.358), channel_id=1, source_target_pairs={{0,1},{1,2},{2,3},{3,0},{4,5},{5,6},{6,7},{7,4},{8,9},{9,10},{10,1... | collective-permute-start | bytes 1592 | tf_op jit(solution)/shard_map/ppermute | solution.py:29
  (78 other events, 476.0 us)
Sparse Core Ops, SparseCore 0:
  545.8 59.8 all-gather.1
where the time goes:
time: 619 us; the launch traced here: 617 us
  blocking collectives  341 us (55%)
  other arithmetic  72.2 us (12%)
  waiting for transfers between devices  71.1 us (11%)
  local copies, waits for them, and re-layouts  59.9 us (10%)
  starting transfers between devices  56.1 us (9%)
  between operations  16.4 us (3%)
    psum x6, blocking collectives, squared_norm(): return lax.psum(member_total(residual * residual), ('gridy', 'gridx'))  187 us
    psum x4, blocking collectives, surface_solve(): lax.psum(member_total(direction * image), ('gridy', 'gridx'))  124 us
    ppermute x24, starting transfers between devices, padded_2(): lax.ppermute(lax.slice_in_dim(block, 0, width, axis=dim), axis, backward)  41.1 us
    ppermute x24, waiting for transfers between devices, padded_2(): lax.ppermute(lax.slice_in_dim(block, block.shape[dim] - width, None, axis...  35.8 us
    all_gather x1, waiting for transfers between devices, shards(): lax.all_gather(state_stack, 'member', axis=1, tiled=True)  23.3 us
    ppermute x24, starting transfers between devices, padded_2(): lax.ppermute(lax.slice_in_dim(block, block.shape[dim] - width, None, axis...  14.9 us
  transfers between devices with their start and end apart: 49, of which 33 were waited for; matrix products, arithmetic and copies ran while one was open for 8% of the time, Pallas kernels for 0%

commit v1 on v0

v1 whole, which is shorter than its diff:
```python
import functools

import jax
import jax.numpy as jnp
from jax import lax
from jax.experimental import pallas as pl
from jax.experimental.pallas import tpu as pltpu
from jax.sharding import PartitionSpec as P

STEPS = 2
ITERS = 3

ALPHA_T = 0.8
BETA_S = 0.6
PRESS_K = 0.25
STEP_DT = 0.1
KAPPA = 0.1
VISCOSITY = 0.1
DRAG_K = 0.05
CORI_K = 1.0
SURF_C = 4.0
DIV_K = 0.5
GRAV_K = 0.5

ADV = STEP_DT * 0.5
DIV = DIV_K * 0.5
GRAV = GRAV_K * 0.5

WIDE = 10
TOP = 24
CHUNK = 16
LANE = 128
PER_GROUP = 11
PAIRS = [(a, b) for a in range(4) for b in range(a, 4)]
SUMS = 6 + 6 * len(PAIRS)
SUM_ROWS = -(-SUMS // 8) * 8
SUM_LANES = SUM_ROWS // 8
VMEM_LIMIT = 56 * 1024 * 1024


def rim_place(plane):
    group, place = divmod(plane, PER_GROUP)
    if place < 6:
        return group, 0, (2 * place + 1) * WIDE
    return group, 1, (2 * (place - 6) + 2) * WIDE


def groups_of(planes):
    return -(-planes // PER_GROUP)


def lanes_like(shape):
    return lax.broadcasted_iota(jnp.int32, shape, len(shape) - 1)


def load_plane(fields, m, plane, levels):
    if plane < 4 * levels:
        return fields[plane // levels][m, plane % levels]
    if plane == 4 * levels:
        return fields[4][m]
    return fields[5][...].astype(jnp.float32)


def pack_kernel(levels, temp, salt, uvel, vvel, eta, mask, to_west, to_east, to_north, to_south, *corners):
    members, _, rows, cols = temp.shape
    planes = 4 * levels + 2
    fields = (temp, salt, uvel, vvel, eta, mask)
    lane = lanes_like((rows, LANE))
    for m in range(members):
        west_parts = [None] * groups_of(planes)
        east_parts = [None] * groups_of(planes)
        for plane in range(planes):
            value = load_plane(fields, m, plane, levels)
            group, _, start = rim_place(plane)
            both = jnp.where(lane < WIDE, value[:, :LANE], value[:, cols - LANE :])
            both = pltpu.roll(both, start, 1)
            is_west = (lane >= start) & (lane < start + WIDE)
            is_east = (lane >= start - WIDE) & (lane < start)
            zero = jnp.zeros_like(both)
            west_parts[group] = jnp.where(is_west, both, zero if west_parts[group] is None else west_parts[group])
            east_parts[group] = jnp.where(is_east, both, zero if east_parts[group] is None else east_parts[group])
            to_south[m, plane * WIDE : (plane + 1) * WIDE, :] = value[:WIDE]
            to_north[m, plane * WIDE : (plane + 1) * WIDE, :] = value[rows - WIDE :]
        for group in range(groups_of(planes)):
            where = slice(group * LANE, (group + 1) * LANE)
            to_west[m, :, where] = west_parts[group]
            to_east[m, :, where] = east_parts[group]
            corners[0][m, :, where] = west_parts[group][:CHUNK]
            corners[1][m, :, where] = west_parts[group][rows - CHUNK :]
            corners[2][m, :, where] = east_parts[group][:CHUNK]
            corners[3][m, :, where] = east_parts[group][rows - CHUNK :]


def whole(count):
    return [pl.BlockSpec(memory_space=pltpu.VMEM)] * count


def pack_rims(temp, salt, uvel, vvel, eta, mask):
    members, levels, rows, cols = temp.shape
    planes = 4 * levels + 2
    wide = groups_of(planes) * LANE
    row_pack = -(-planes * WIDE // 8) * 8
    side = jax.ShapeDtypeStruct((members, rows, wide), jnp.float32)
    line = jax.ShapeDtypeStruct((members, row_pack, cols), jnp.float32)
    corner = jax.ShapeDtypeStruct((members, CHUNK, wide), jnp.float32)
    return pl.pallas_call(
        functools.partial(pack_kernel, levels),
        out_shape=(side, side, line, line, corner, corner, corner, corner),
        in_specs=whole(6),
        out_specs=tuple(whole(8)),
        compiler_params=pltpu.CompilerParams(vmem_limit_bytes=VMEM_LIMIT),
        name="pack_rims",
    )(temp, salt, uvel, vvel, eta, mask)


def east_west(value):
    width = value.shape[-1]
    return pltpu.roll(value, width - 1, 1), pltpu.roll(value, 1, 1)


def chunks(first, last):
    return [(a, min(a + CHUNK, last)) for a in range(first, last, CHUNK)]


def assemble(ext, fields, rims, m, levels):
    from_east, from_west, from_north, from_south, ne, nw, se, sw = rims
    planes = 4 * levels + 2
    rows, cols = fields[5].shape
    bands = [(TOP - CHUNK, se, sw, 0, CHUNK)]
    bands += [(TOP + a, from_east, from_west, a, CHUNK) for a in range(0, rows, CHUNK)]
    bands += [(TOP + rows, ne, nw, 0, CHUNK)]
    for group in range(groups_of(planes)):
        where = slice(group * LANE, (group + 1) * LANE)
        for at, east_ref, west_ref, start, size in bands:
            east = east_ref[m, start : start + size, where]
            west = west_ref[m, start : start + size, where]
            slot = lanes_like(east.shape) // WIDE
            odd = (slot & 1) == 1
            joined = (jnp.where(odd, east, west), jnp.where(odd, west, east))
            for plane in range(group * PER_GROUP, min((group + 1) * PER_GROUP, planes)):
                _, kind, offset = rim_place(plane)
                ext[plane, at : at + size, cols : cols + LANE] = pltpu.roll(joined[kind], LANE - offset, 1)
    for plane in range(planes):
        ext[plane, TOP : TOP + rows, :cols] = load_plane(fields, m, plane, levels)
        ext[plane, TOP - WIDE : TOP, :cols] = from_south[m, plane * WIDE : (plane + 1) * WIDE, :]
        ext[plane, TOP + rows : TOP + rows + WIDE, :cols] = from_north[m, plane * WIDE : (plane + 1) * WIDE, :]


def fill_rows(cor, inside, first_row, total_rows):
    shape = (CHUNK, cor.shape[1])
    for a in range(0, cor.shape[0], CHUNK):
        row = first_row + (a - TOP) + lax.broadcasted_iota(jnp.int32, shape, 0)
        latitude = row.astype(jnp.float32) + 0.5
        cor[a : a + CHUNK, :] = CORI_K * (2.0 * latitude / total_rows - 1.0)
        inside[a : a + CHUNK, :] = jnp.where((row >= 0) & (row < total_rows), 1.0, 0.0)


class Planes:
    def __init__(self, ref, names):
        self.ref, self.names = ref, names

    def get(self, name, a, b):
        return self.ref[self.names.index(name), a:b, :]

    def put(self, name, a, b, value):
        self.ref[self.names.index(name), a:b, :] = value

    def sides(self, name, a, b):
        here = self.get(name, a, b)
        east, west = east_west(here)
        return here, east, west, self.get(name, a + 1, b + 1), self.get(name, a - 1, b - 1)

    def lap(self, name, a, b):
        here, east, west, north, south = self.sides(name, a, b)
        return east + west + north + south - 4.0 * here


def momentum(ocean, cor, u, v, pu, pv, lap_u, lap_v):
    new_u = ocean * (u + STEP_DT * (cor * v - 0.5 * pu - DRAG_K * u) + VISCOSITY * lap_u)
    new_v = ocean * (v + STEP_DT * (-cor * u - 0.5 * pv - DRAG_K * v) + VISCOSITY * lap_v)
    return new_u, new_v


def surface_start(ext, work, cor, inside, levels, rows):
    ocean_at = 4 * levels + 1
    low, high = TOP - CHUNK, TOP + rows + CHUNK
    near_low, near_high = TOP - 8, TOP + rows + 8
    for a, b in chunks(low, high):
        su = sv = sp = None
        for l in range(levels):
            dens = BETA_S * ext[levels + l, a:b, :] - ALPHA_T * ext[l, a:b, :]
            work.put("d%d" % l, a, b, dens)
            u, v = ext[2 * levels + l, a:b, :], ext[3 * levels + l, a:b, :]
            weighted = (PRESS_K * (levels - l)) * dens
            su, sv, sp = (u, v, weighted) if l == 0 else (su + u, sv + v, sp + weighted)
        work.put("su", a, b, su)
        work.put("sv", a, b, sv)
        work.put("sp", a, b, sp)
    for a, b in chunks(near_low, near_high):
        carried = None
        for l in range(levels):
            _, east, west, north, south = work.sides("d%d" % l, a, b)
            term = ext[2 * levels + l, a:b, :] * (east - west) + ext[3 * levels + l, a:b, :] * (north - south)
            term = (PRESS_K * (levels - l)) * term
            carried = term if l == 0 else carried + term
        here, east, west, north, south = work.sides("sp", a, b)
        lap = east + west + north + south - 4.0 * here
        work.put("q", a, b, ext[ocean_at, a:b, :] * (here - ADV * carried + KAPPA * lap))
    for a, b in chunks(low, high):
        ocean = ext[ocean_at, a:b, :]
        _, pe, pw, pn, ps = work.sides("sp", a, b)
        new_u, new_v = momentum(
            ocean, cor[a:b, :], work.get("su", a, b), work.get("sv", a, b),
            pe - pw, pn - ps, work.lap("su", a, b), work.lap("sv", a, b),
        )
        work.put("tu", a, b, new_u)
        work.put("tv", a, b, new_v)
    for a, b in chunks(near_low, near_high):
        work.put("v0", a, b, inside[a:b, :] * (ext[4 * levels, a:b, :] - divergence(work, "tu", "tv", a, b)))


def divergence(work, u_name, v_name, a, b):
    east, west = east_west(work.get(u_name, a, b))
    return DIV * (east - west + (work.get(v_name, a + 1, b + 1) - work.get(v_name, a - 1, b - 1)))


def around(work, name, a, b):
    _, east, west, north, south = work.sides(name, a, b)
    return east + west + north + south


def powers(work, inside, first, second, third, low, high):
    for a, b in chunks(low, high):
        work.put(second, a, b, inside[a:b, :] * around(work, first, a, b))
    for a, b in chunks(low, high):
        work.put(third, a, b, inside[a:b, :] * (around(work, second, a, b) - 4.0 * work.get(first, a, b)))


def surface_next(work, ext, cor, inside, levels, rows, u_name, v_name, eta_name, with_press, out_name):
    low, high = TOP - 8, TOP + rows + 8
    ocean_at = 4 * levels + 1
    for a, b in chunks(low, high):
        if with_press:
            _, pe, pw, pn, ps = work.sides("q", a, b)
            pu, pv = pe - pw, pn - ps
        else:
            pu = pv = 0.0
        new_u, new_v = momentum(
            ext[ocean_at, a:b, :], cor[a:b, :], work.get(u_name, a, b), work.get(v_name, a, b),
            pu, pv, work.lap(u_name, a, b), work.lap(v_name, a, b),
        )
        work.put("t2u", a, b, new_u)
        work.put("t2v", a, b, new_v)
    for a, b in chunks(low, high):
        div = divergence(work, "t2u", "t2v", a, b)
        value = -div if eta_name is None else work.get(eta_name, a, b) - div
        work.put(out_name, a, b, inside[a:b, :] * value)


def surface_push(work, ext, levels, rows, eta_name, u_name, v_name, base):
    ocean_at = 4 * levels + 1
    for a, b in chunks(TOP - 8, TOP + rows + 8):
        ocean = ext[ocean_at, a:b, :]
        _, east, west, north, south = work.sides(eta_name, a, b)
        push_u = -(levels * GRAV) * ocean * (east - west)
        push_v = -(levels * GRAV) * ocean * (north - south)
        if base:
            push_u, push_v = work.get("tu", a, b) + push_u, work.get("tv", a, b) + push_v
        work.put(u_name, a, b, push_u)
        work.put(v_name, a, b, push_v)


SUM_NAMES = ["d0", "d1", "d2", "d3", "su", "sv", "sp", "q", "tu", "tv", "v0", "v1", "v2", "v3", "pu", "pv", "t2u", "t2v"]
SUM_NAMES += ["w%d_%d" % (i, k) for i in range(4) for k in range(4)]


def sums_kernel(levels, total_rows, place, *refs):
    fields, rims, out, scratch = refs[:6], refs[6:14], refs[14], refs[15:]
    ext, planes, cor, inside, red = scratch
    members = fields[0].shape[0]
    rows, cols = fields[5].shape
    work = Planes(planes, SUM_NAMES)
    fill_rows(cor, inside, place[0], total_rows)
    red[...] = jnp.zeros_like(red)

    def one(m, carry):
        assemble(ext, fields, rims, m, levels)
        surface_start(ext, work, cor, inside, levels, rows)
        low, high = TOP - 8, TOP + rows + 8
        powers(work, inside, "v0", "v1", "v2", low, high)
        for a, b in chunks(TOP, TOP + rows):
            work.put("v3", a, b, around(work, "v2", a, b))
        surface_next(work, ext, cor, inside, levels, rows, "tu", "tv", None, True, "w0_0")
        for k in range(1, 4):
            name = "v%d" % (k - 1)
            surface_push(work, ext, levels, rows, name, "pu", "pv", False)
            surface_next(work, ext, cor, inside, levels, rows, "pu", "pv", name, False, "w0_%d" % k)
        for k in range(4):
            powers(work, inside, "w0_%d" % k, "w1_%d" % k, "w2_%d" % k, low, high)
            for a, b in chunks(TOP, TOP + rows):
                work.put("w3_%d" % k, a, b, around(work, "w2_%d" % k, a, b))

        def put_sum(at, first, second):
            total = None
            for a, b in chunks(TOP, TOP + rows):
                x = planes[SUM_NAMES.index(first), a:b, :cols]
                y = planes[SUM_NAMES.index(second), a:b, :cols]
                total = x * y if total is None else total + x * y
            line = jnp.sum(total, axis=0, keepdims=True)
            folded = line[:, :LANE]
            for c in range(LANE, cols, LANE):
                folded = folded + line[:, c : c + LANE]
            red[m, at : at + 1, :] = folded

        for i in range(6):
            put_sum(i, "v%d" % (i // 2), "v%d" % (i - i // 2))
            for p, (a, b) in enumerate(PAIRS):
                put_sum(6 + i * len(PAIRS) + p, "w%d_%d" % (i // 2, a), "w%d_%d" % (i - i // 2, b))
        return carry

    lax.fori_loop(0, members, one, 0)
    lane = lanes_like((8, LANE))
    tile = jnp.zeros((8, LANE), jnp.float32)
    for m in range(members):
        total = jnp.sum(red[m], axis=1, keepdims=True)
        for q in range(SUM_LANES):
            tile = jnp.where(lane == m * SUM_LANES + q, total[8 * q : 8 * q + 8], tile)
    out[...] = tile


def plane_shape(rows, cols):
    return (2 * TOP + rows, cols + LANE)


def local_sums(place, fields, rims, total_rows):
    members, levels, rows, cols = fields[0].shape
    shape = plane_shape(rows, cols)
    return pl.pallas_call(
        functools.partial(sums_kernel, levels, total_rows),
        out_shape=jax.ShapeDtypeStruct((8, LANE), jnp.float32),
        in_specs=[pl.BlockSpec(memory_space=pltpu.SMEM)] + whole(14),
        out_specs=pl.BlockSpec(memory_space=pltpu.VMEM),
        scratch_shapes=[
            pltpu.VMEM((4 * levels + 2,) + shape, jnp.float32),
            pltpu.VMEM((len(SUM_NAMES),) + shape, jnp.float32),
            pltpu.VMEM(shape, jnp.float32),
            pltpu.VMEM(shape, jnp.float32),
            pltpu.VMEM((members, SUM_ROWS, LANE), jnp.float32),
        ],
        compiler_params=pltpu.CompilerParams(vmem_limit_bytes=VMEM_LIMIT),
        name="local_sums",
    )(place, *fields, *rims)


def krylov(moment):
    n00, n01, n11, n12, n22, x22 = moment
    n02 = n11 - 4.0 * n00
    main, near = 1.0 + 4.0 * SURF_C, SURF_C
    g00 = main * n00 - near * n01
    g01 = main * n01 - near * n11
    g02 = main * n02 - near * n12
    g11 = main * n11 - near * (n12 + 4.0 * n01)
    g12 = main * n12 - near * (n22 + 4.0 * n02)
    g22 = main * n22 - near * x22
    l1, l2 = g01 / g00, g02 / g00
    d1 = g11 - l1 * g01
    d1 = jnp.where(d1 > 3e-7 * g11, d1, jnp.inf)
    e = g12 - l1 * g02
    l12 = e / d1
    d2 = g22 - l2 * g02 - l12 * e
    d2 = jnp.where(d2 > 3e-7 * g22, d2, jnp.inf)
    z0 = n00
    z1 = n01 - l1 * z0
    z2 = n02 - l2 * z0 - l12 * z1
    y2 = z2 / d2
    y1 = z1 / d1 - l12 * y2
    y0 = z0 / g00 - l1 * y1 - l2 * y2
    return [y0, y1, y2]


def weights(read):
    first = krylov([read(i) for i in range(6)])
    lifted = [None] + first
    second = []
    for i in range(6):
        total = None
        for p, (a, b) in enumerate(PAIRS):
            term = read(6 + i * len(PAIRS) + p)
            for k in (a, b):
                if k:
                    term = term * lifted[k]
            if a != b:
                term = 2.0 * term
            total = term if total is None else total + term
        second.append(total)
    return first, krylov(second)


RUN_NAMES = ["d0", "d1", "d2", "d3", "su", "sv", "sp", "q", "tu", "tv", "v0", "v1", "v2", "pu", "pv", "t2u", "t2v"]
RUN_NAMES += ["eta1", "w0", "w1", "w2", "eta2", "p", "p2"]


def combine(work, factors, names, out_name, a, b):
    total = None
    for factor, name in zip(factors, names):
        term = factor * work.get(name, a, b)
        total = term if total is None else total + term
    work.put(out_name, a, b, total)


def advance_kernel(levels, total_rows, place, sums, *refs):
    fields, rims = refs[:6], refs[6:14]
    new_temp, new_salt, new_uvel, new_vvel, new_eta, zonal = refs[14:20]
    ext, planes, after, cor, inside = refs[20:]
    members = fields[0].shape[0]
    rows, cols = fields[5].shape
    ocean_at = 4 * levels + 1
    work = Planes(planes, RUN_NAMES)
    fill_rows(cor, inside, place[0], total_rows)
    zonal[...] = jnp.zeros_like(zonal)
    low, high = TOP - 8, TOP + rows + 8

    def one(m, carry):
        assemble(ext, fields, rims, m, levels)

        def read(i):
            return jnp.full((1, 1), sums[i % 8, m * SUM_LANES + i // 8], jnp.float32)

        first, second = weights(read)
        surface_start(ext, work, cor, inside, levels, rows)
        powers(work, inside, "v0", "v1", "v2", low, high)
        for a, b in chunks(low, high):
            combine(work, first, ("v0", "v1", "v2"), "eta1", a, b)
        surface_push(work, ext, levels, rows, "eta1", "pu", "pv", True)
        surface_next(work, ext, cor, inside, levels, rows, "pu", "pv", "eta1", True, "w0")
        powers(work, inside, "w0", "w1", "w2", low, high)
        for a, b in chunks(low, high):
            combine(work, second, ("w0", "w1", "w2"), "eta2", a, b)
        for a, b in chunks(TOP, TOP + rows):
            new_eta[m, a - TOP : b - TOP, :] = work.get("eta2", a, b)[:, :cols]
        for a, b in chunks(low, high):
            ocean = ext[ocean_at, a:b, :]
            for name, to_u, to_v in (("eta1", "pu", "pv"), ("eta2", "t2u", "t2v")):
                _, east, west, north, south = work.sides(name, a, b)
                work.put(to_u, a, b, GRAV * ocean * (east - west))
                work.put(to_v, a, b, GRAV * ocean * (north - south))
        for a, b in chunks(TOP - CHUNK, TOP + rows + CHUNK):
            work.put("p", a, b, jnp.zeros((b - a, cols + LANE), jnp.float32))
            work.put("p2", a, b, jnp.zeros((b - a, cols + LANE), jnp.float32))

        def sides(ref, at, a, b):
            here = ref[at, a:b, :]
            east, west = east_west(here)
            north, south = ref[at, a + 1 : b + 1, :], ref[at, a - 1 : b - 1, :]
            return here, east - west, north - south, east + west + north + south - 4.0 * here

        def step(ref, l, press, a, b):
            ocean = ext[ocean_at, a:b, :]
            temp, temp_x, temp_y, temp_l = sides(ref, l, a, b)
            salt, salt_x, salt_y, salt_l = sides(ref, levels + l, a, b)
            u, _, _, u_l = sides(ref, 2 * levels + l, a, b)
            v, _, _, v_l = sides(ref, 3 * levels + l, a, b)
            _, pe, pw, pn, ps = work.sides(press, a, b)
            temp = ocean * (temp - ADV * (u * temp_x + v * temp_y) + KAPPA * temp_l)
            salt = ocean * (salt - ADV * (u * salt_x + v * salt_y) + KAPPA * salt_l)
            u, v = momentum(ocean, cor[a:b, :], u, v, pe - pw, pn - ps, u_l, v_l)
            return temp, salt, u, v

        def add_press(ref, l, press, a, b):
            dens = BETA_S * ref[levels + l, a:b, :] - ALPHA_T * ref[l, a:b, :]
            work.put(press, a, b, work.get(press, a, b) + PRESS_K * dens)

        def level(l, carry):
            for a, b in chunks(TOP - CHUNK, TOP + rows + CHUNK):
                add_press(ext, l, "p", a, b)
            for a, b in chunks(low, high):
                temp, salt, u, v = step(ext, l, "p", a, b)
                after[l, a:b, :] = temp
                after[levels + l, a:b, :] = salt
                after[2 * levels + l, a:b, :] = u - work.get("pu", a, b)
                after[3 * levels + l, a:b, :] = v - work.get("pv", a, b)
            for a, b in chunks(low, high):
                add_press(after, l, "p2", a, b)
            for a, b in chunks(TOP, TOP + rows):
                temp, salt, u, v = step(after, l, "p2", a, b)
                u = u - work.get("t2u", a, b)
                v = v - work.get("t2v", a, b)
                here = slice(a - TOP, b - TOP)
                new_temp[m, l, here, :] = temp[:, :cols]
                new_salt[m, l, here, :] = salt[:, :cols]
                new_uvel[m, l, here, :] = u[:, :cols]
                new_vvel[m, l, here, :] = v[:, :cols]
                total = jnp.sum(v[:, :cols], axis=1, keepdims=True)
                lane = lanes_like((b - a, LANE))
                zonal[here, :] = jnp.where(lane == m * levels + l, total, zonal[here, :])
            return carry

        lax.fori_loop(0, levels, level, 0)
        return carry

    lax.fori_loop(0, members, one, 0)


def advance(place, sums, fields, rims, total_rows):
    members, levels, rows, cols = fields[0].shape
    shape = plane_shape(rows, cols)
    volume = jax.ShapeDtypeStruct((members, levels, rows, cols), jnp.float32)
    surface = jax.ShapeDtypeStruct((members, rows, cols), jnp.float32)
    return pl.pallas_call(
        functools.partial(advance_kernel, levels, total_rows),
        out_shape=(volume,) * 4 + (surface, jax.ShapeDtypeStruct((rows, LANE), jnp.float32)),
        in_specs=[pl.BlockSpec(memory_space=pltpu.SMEM)] * 2 + whole(14),
        out_specs=tuple(whole(6)),
        scratch_shapes=[
            pltpu.VMEM((4 * levels + 2,) + shape, jnp.float32),
            pltpu.VMEM((len(RUN_NAMES),) + shape, jnp.float32),
            pltpu.VMEM((4 * levels,) + shape, jnp.float32),
            pltpu.VMEM(shape, jnp.float32),
            pltpu.VMEM(shape, jnp.float32),
        ],
        compiler_params=pltpu.CompilerParams(vmem_limit_bytes=VMEM_LIMIT),
        name="advance",
    )(place, sums, *fields, *rims)


def exchange_rims(packed):
    to_west, to_east, to_north, to_south, west_low, west_high, east_low, east_high = packed
    count_y, count_x = lax.axis_size("gridy"), lax.axis_size("gridx")

    def move(value, north, east):
        pairs = []
        for j in range(count_y):
            for i in range(count_x):
                if 0 <= j + north < count_y:
                    pairs.append((j * count_x + i, (j + north) * count_x + (i + east) % count_x))
        return lax.ppermute(value, ("gridy", "gridx"), pairs)

    return (
        move(to_west, 0, -1),
        move(to_east, 0, 1),
        move(to_south, -1, 0),
        move(to_north, 1, 0),
        move(west_low, -1, -1),
        move(east_low, -1, 1),
        move(west_high, 1, -1),
        move(east_high, 1, 1),
    )


def total_over(value, axis):
    count = lax.axis_size(axis)
    if count <= 4:
        moved = [
            lax.ppermute(value, axis, [(i, (i + shift) % count) for i in range(count)]) for shift in range(1, count)
        ]
        for part in moved:
            value = value + part
        return value
    step = 1
    while step < count:
        if count % (2 * step):
            return lax.psum(value, axis)
        value = value + lax.ppermute(value, axis, [(i, i ^ step) for i in range(count)])
        step *= 2
    return value


def swap_members(value):
    return lax.all_gather(value, "member", axis=0, tiled=True)


def shards(temp, salt, uvel, vvel, eta, land_mask, clone_source):
    members, levels, rows, cols = temp.shape
    tile_row = lax.axis_index("gridy")
    total_rows = rows * lax.axis_size("gridy")
    total_cols = cols * lax.axis_size("gridx")
    place = (tile_row * rows).astype(jnp.int32).reshape(1)
    fields = (temp, salt, uvel, vvel, eta, land_mask)
    rims = exchange_rims(pack_rims(*fields))
    sums = local_sums(place, fields, rims, total_rows)
    sums = total_over(total_over(sums, "gridx"), "gridy")
    *state, zonal = advance(place, sums, fields, rims, total_rows)
    side = lax.axis_index("member")
    count = lax.axis_size("member")
    every = [lax.all_gather(value, "member", axis=0, tiled=True) for value in state]
    picked = [jnp.take(value, clone_source, axis=0) for value in every]

    zonal_whole = total_over(zonal, "gridx")[:, : members * levels].reshape(rows, members, levels)
    zonal_whole = jnp.transpose(zonal_whole, (1, 2, 0))
    zonal_scale = 1.0 / jnp.sqrt(jnp.float32(total_cols))
    score_scale = 1.0 / jnp.sqrt(jnp.float32(levels * total_rows))
    latitude = (tile_row * rows + jnp.arange(rows, dtype=jnp.int32)).astype(jnp.float32) + 0.5
    overturn = jnp.cumsum(zonal_whole, axis=1) * zonal_scale
    score = total_over(jnp.sum(overturn * (latitude / total_rows), axis=(1, 2)) * score_scale, "gridy")
    every_score = lax.all_gather(score, "member", axis=0, tiled=True)
    clone_weight = jnp.take(every_score, clone_source, axis=0) - jnp.mean(every_score)
    return (*picked, overturn, clone_weight)


def solution(mesh):
    volume = P("member", None, "gridy", "gridx")
    in_specs = (volume,) * 4 + (P("member", "gridy", "gridx"), P("gridy", "gridx"), P("member"))
    out_specs = (volume,) * 4 + (P("member", "gridy", "gridx"), P("member", None, "gridy"), P("member"))
    return jax.shard_map(shards, mesh=mesh, in_specs=in_specs, out_specs=out_specs, check_vma=False)
```

time: 619 us -> 189 us (0.31)
  blocking collectives: 341 us -> 14.2 us
  other arithmetic: 72.2 us -> 5.39 us
  local copies, waits for them, and re-layouts: 59.9 us -> 11.2 us
  Pallas kernels: 0 us -> 27.7 us
  starting transfers between devices: 56.1 us -> 36.1 us
  waiting for transfers between devices: 71.1 us -> 78.2 us
    psum x12 -> x0, blocking collectives: 328 us -> none  [the longest x6 187 us: squared_norm(): return lax.psum(member_total(residual * residual), ('gridy', 'gridx'))]
    all_gather x1 -> x4, waiting for transfers between devices: 23.3 us -> 58.1 us  [shards(): lax.all_gather(value, 'member', axis=0, tiled=True)]
    ppermute x48 -> x20, waiting for transfers between devices: 47.8 us -> 18.7 us  [the longest x8 14.2 us: move(): return lax.ppermute(value, ('gridy', 'gridx'), pairs)]
    pallas_call x0 -> x3, Pallas kernels: none -> 27.7 us  [the longest x1 15.4 us: advance(): pl.pallas_call(functools.partial(advance_kernel, levels, total_rows), out...]
    reduce_sum x15 -> x0, other arithmetic: 26.3 us -> none  [the longest x10 10.8 us: member_total(): return jnp.sum(values, axis=(1, 2))]
    another operation x24 -> x0, local copies, waits for them, and re-layouts: 22 us -> none  [the longest x12 12 us: split_rims(): south_side = south_side.at[..., 0, :].multiply(south_keep)]
    ppermute x48 -> x20, starting transfers between devices: 56 us -> 35.9 us  [the longest x12 18.1 us: total_over(): lax.ppermute(value, axis, [(i, (i + shift) % count) for i in range(count)])]
    slice x26 -> x1, local copies, waits for them, and re-layouts: 16.5 us -> 0.06 us  [shards(): total_over(zonal, 'gridx')[:, :members * levels]]
  transfers between devices with their start and end apart: 49 -> 24, of which waited for: 33 -> 14; matrix products, arithmetic and copies ran while one was open for 8% -> 5% of each run, Pallas kernels for 0% -> 0%
where the time goes in v1:
time: 189 us; the launch traced here: 188 us
  waiting for transfers between devices  78.2 us (41%)
  starting transfers between devices  36.1 us (19%)
  Pallas kernels  27.7 us (15%)
  between operations  15.3 us (8%)
  blocking collectives  14.2 us (8%)
  local copies, waits for them, and re-layouts  11.2 us (6%)
  other arithmetic  5.39 us (3%)
    all_gather x4, waiting for transfers between devices, shards(): lax.all_gather(value, 'member', axis=0, tiled=True)  58.1 us
    ppermute x12, starting transfers between devices, total_over(): lax.ppermute(value, axis, [(i, (i + shift) % count) for i in range(count)])  18.1 us
    ppermute x8, starting transfers between devices, move(): return lax.ppermute(value, ('gridy', 'gridx'), pairs)  17.8 us
    pallas_call x1, Pallas kernels, advance(): pl.pallas_call(functools.partial(advance_kernel, levels, total_rows), out...  15.4 us
    ppermute x8, waiting for transfers between devices, move(): return lax.ppermute(value, ('gridy', 'gridx'), pairs)  14.2 us
    pallas_call x1, Pallas kernels, local_sums(): pl.pallas_call(functools.partial(sums_kernel, levels, total_rows), out_sh...  9.51 us
    all_gather x1, blocking collectives, shards(): lax.all_gather(value, 'member', axis=0, tiled=True)  9.3 us
    gather x5, local copies, waits for them, and re-layouts, shards(): picked = [jnp.take(value, clone_source, axis=0) for value in every]  7.78 us
  transfers between devices with their start and end apart: 24, of which 14 were waited for; matrix products, arithmetic and copies ran while one was open for 5% of the time, Pallas kernels for 0%

profile of v1, /device:TPU:0, one launch (start us, length us, event | category | flops | bytes accessed | tf_op | source)
XLA Modules:
  0.0 188.2 jit_solution(8995810366861227611)
XLA Ops:
  7.2 2.8 %pack_rims.1 = (f32[2,64,256]{2,1,0:T(8,128)}, f32[2,64,256]{2,1,0:T(8,128)}, f32[2,184,256]{2,1,0:T(8,128)}, f32[2,184,256]{2,1,0:T(8,128)}, f32[2,16,256]{2,1,...) custom-call(f32[2,4,64,256]{3,2,1,0:T(8,128)} %refs_0_.3, ...), custom_call_target="tpu_custom_call" | custom-call | tf_op jit(solution)/shard_map/pack_rims/pallas_call | solution.py:106
  11.3 3.1 %collective-permute-start.3 = (f32[2,184,256]{2,1,0:T(8,128)}, f32[2,184,256]{2,1,0:T(8,128)S(1)}, u32[]{:S(2)}, u32[]{:S(2)}) collective-permute-start(f32[2,184,256]{2,1,0:T(8,128)} %get-tuple-element.25), channel_id=1, source_target_pairs={{0,4},{1,5},{2,6},{3,7},{4,8},{5,9},{6,10},{7,11},{8,12},{9,13},{1... | collective-permute-start | bytes 1130504 | tf_op jit(solution)/shard_map/ppermute | solution.py:536
  15.6 5.1 %collective-permute-start = (f32[2,64,256]{2,1,0:T(8,128)}, f32[2,64,256]{2,1,0:T(8,128)S(1)}, u32[]{:S(2)}, u32[]{:S(2)}) collective-permute-start(f32[2,64,256]{2,1,0:T(8,128)} %get-tuple-element.22), channel_id=1, source_target_pairs={{0,3},{1,0},{2,1},{3,2},{4,7},{5,4},{6,5},{7,6},{8,11},{9,8},{10,9... | collective-permute-start | bytes 393224 | tf_op jit(solution)/shard_map/ppermute | solution.py:536
  23.4 9.1 %collective-permute-done.5.refs_11_ = f32[2,16,256]{2,1,0:T(8,128)S(1)} collective-permute-done((f32[2,16,256]{2,1,0:T(8,128)}, f32[2,16,256]{2,1,0:T(8,128)S(1)}, u32[]{:S(2)}, u32[]{:S(2)}) %collective-permute-start.5) | collective-permute-done | bytes 32800 | tf_op jit(solution)/shard_map/ppermute | solution.py:536
  32.5 4.5 %collective-permute-start.6 = (f32[2,16,256]{2,1,0:T(8,128)}, f32[2,16,256]{2,1,0:T(8,128)S(1)}, u32[]{:S(2)}, u32[]{:S(2)}) collective-permute-start(f32[2,16,256]{2,1,0:T(8,128)} %get-tuple-element.28), channel_id=1, source_target_pairs={{0,7},{1,4},{2,5},{3,6},{4,11},{5,8},{6,9},{7,10},{8,15},{9,12},{1... | collective-permute-start | bytes 98312 | tf_op jit(solution)/shard_map/ppermute | solution.py:536
  37.0 1.9 %collective-permute-done.6.refs_12_ = f32[2,16,256]{2,1,0:T(8,128)S(1)} collective-permute-done((f32[2,16,256]{2,1,0:T(8,128)}, f32[2,16,256]{2,1,0:T(8,128)S(1)}, u32[]{:S(2)}, u32[]{:S(2)}) %collective-permute-start.6) | collective-permute-done | bytes 32800 | tf_op jit(solution)/shard_map/ppermute | solution.py:536
  40.2 1.9 %collective-permute-done.7.refs_13_ = f32[2,16,256]{2,1,0:T(8,128)S(1)} collective-permute-done((f32[2,16,256]{2,1,0:T(8,128)}, f32[2,16,256]{2,1,0:T(8,128)S(1)}, u32[]{:S(2)}, u32[]{:S(2)}) %collective-permute-start.7) | collective-permute-done | bytes 32800 | tf_op jit(solution)/shard_map/ppermute | solution.py:536
  43.0 9.5 %local_sums.1 = f32[8,128]{1,0:T(8,128)} custom-call(s32[1]{0:T(128)} %bitcast.place, f32[2,4,64,256]{3,2,1,0:T(8,128)} %refs_0_.3, f32[2,4,64,256]{3,2,1,0:T(8,128)} %refs_1_.3, f32[2,4,64,256]{3,2,1,0:T(8,128)} %refs_2_.3, f32[2,4,64,256]{3,2,1,0:T(8,128)} %refs_3_.3, f32[2,64,256]{2,1,0:T(8,128)} %refs_4_.3, s32[64,256]{1,0:T(8,128)} %refs_5_.3, ...), custom_call_target="tpu_custom_call" | custom-call | tf_op jit(solution)/shard_map/local_sums/pallas_call | solution.py:338
  52.5 2.0 %collective-permute-start.10 = (f32[8,128]{1,0:T(8,128)}, f32[8,128]{1,0:T(8,128)S(1)}, u32[]{:S(2)}, u32[]{:S(2)}) collective-permute-start(f32[8,128]{1,0:T(8,128)} %local_sums.1), channel_id=1, source_target_pairs={{0,3},{1,0},{2,1},{3,2},{4,7},{5,4},{6,5},{7,6},{8,11},{9,8},{10,9... | collective-permute-start | bytes 12296 | tf_op jit(solution)/shard_map/ppermute | solution.py:554
  54.6 4.6 %collective-permute-start.9 = (f32[8,128]{1,0:T(8,128)}, f32[8,128]{1,0:T(8,128)S(1)}, u32[]{:S(2)}, u32[]{:S(2)}) collective-permute-start(f32[8,128]{1,0:T(8,128)} %local_sums.1), channel_id=1, source_target_pairs={{0,2},{1,3},{2,0},{3,1},{4,6},{5,7},{6,4},{7,5},{8,10},{9,11},{10,... | collective-permute-start | bytes 12296 | tf_op jit(solution)/shard_map/ppermute | solution.py:554
  61.7 1.8 collective-permute-start.11
  63.5 1.9 %collective-permute-start.12 = (f32[8,128]{1,0:T(8,128)S(1)}, f32[8,128]{1,0:T(8,128)S(1)}, u32[]{:S(2)}, u32[]{:S(2)}) collective-permute-start(f32[8,128]{1,0:T(8,128)S(1)} %add_add_fusion.1), channel_id=1, source_target_pairs={{0,8},{4,12},{8,0},{12,4},{1,9},{5,13},{9,1},{13,5},{2,10},{6,14},... | collective-permute-start | bytes 12296 | tf_op jit(solution)/shard_map/ppermute | solution.py:554
  68.8 15.4 %advance.1 = (f32[2,4,64,256]{3,2,1,0:T(8,128)}, f32[2,4,64,256]{3,2,1,0:T(8,128)}, f32[2,4,64,256]{3,2,1,0:T(8,128)}, f32[2,4,64,256]{3,2,1,0:T(8,128)}, f32[2,64,256]{2,1,0:T(8,128)}, /*index=5*/f32[64,128]{1,0:T(8,128)}) custom-call(s32[1]{0:T(128)} %bitcast.place, f32[8,128]{1,0:T(8,128)} %add_add_fusion.sums, f32[2,4,64,256]{3,2,1,0:T(8,128)} %refs_0_.3, ...), custom_call_target="tpu_custom_call" | custom-call | tf_op jit(solution)/shard_map/advance/pallas_call | solution.py:509
  88.5 2.9 %collective-permute-start.15 = (f32[64,128]{1,0:T(8,128)S(1)}, f32[64,128]{1,0:T(8,128)S(1)}, u32[]{:S(2)}, u32[]{:S(2)}) collective-permute-start(f32[64,128]{1,0:T(8,128)S(1)} %copy-done.9), channel_id=1, source_target_pairs={{0,2},{1,3},{2,0},{3,1},{4,6},{5,7},{6,4},{7,5},{8,10},{9,11},{10,... | collective-permute-start | bytes 98312 | tf_op jit(solution)/shard_map/ppermute | solution.py:554
  92.3 9.3 %all_gather.22 = f32[4,64,256]{2,1,0:T(8,128)S(1)} all-gather(f32[2,64,256]{2,1,0:T(8,128)S(1)} %copy-done.8), channel_id=1, replica_groups=mesh['member'=2,'gridy'=4,'gridx'=4] {'member'}, dimensions={0}, use_global_device_ids=true | all-gather | bytes 393216 | tf_op jit(solution)/shard_map/all_gather | solution.py:585
  106.7 4.9 %all-reduce = f32[4]{0:T(128)S(1)} all-reduce(f32[4]{0:T(128)S(1)} %add_dynamic-update-slice_fusion), channel_id=1, replica_groups=mesh['member'=2,'gridy'=4,'gridx'=4] {'member'}, use_global_device_ids=true, to_apply=%add | all-reduce | flops 4 | bytes 32
  114.8 1.8 gather_fusion.2
  116.7 14.9 %all-gather.7.cloned.1.call-done = f32[4,4,64,256]{3,2,1,0:T(8,128)} async-done(((f32[2,4,64,256]{3,2,1,0:T(8,128)}), f32[4,4,64,256]{3,2,1,0:T(8,128)}) %all-gather.7.cloned.1.call-update) | async-done | bytes 1048592 | tf_op jit(solution)/shard_map/all_gather | solution.py:585
  131.6 1.8 gather_fusion.3
  133.4 21.7 %all-gather.9.cloned.1.call-done = f32[4,4,64,256]{3,2,1,0:T(8,128)} async-done(((f32[2,4,64,256]{3,2,1,0:T(8,128)}), f32[4,4,64,256]{3,2,1,0:T(8,128)}) %all-gather.9.cloned.1.call-update) | async-done | bytes 1048592 | tf_op jit(solution)/shard_map/all_gather | solution.py:585
  155.1 1.8 gather_fusion.4
  156.9 21.5 %all-gather.11.cloned.1.call-done = f32[4,4,64,256]{3,2,1,0:T(8,128)} async-done(((f32[2,4,64,256]{3,2,1,0:T(8,128)}), f32[4,4,64,256]{3,2,1,0:T(8,128)}) %all-gather.11.cloned.1.call-update) | async-done | bytes 1048592 | tf_op jit(solution)/shard_map/all_gather | solution.py:585
  178.4 1.8 gather_fusion.5
  180.2 1.5 broadcast_select_fusion
  (80 shorter events, 25.4 us)
Async XLA Ops:
  7.2 107.7 %all-gather.5.cloned.1.call-start = ((), (), s32[]{:S(2)}) async-start(), calls=%async_computation | async-start | bytes 1572864 | tf_op jit(solution)/shard_map/all_gather | solution.py:585
  10.0 32.1 %collective-permute-start.2 = (f32[2,184,256]{2,1,0:T(8,128)}, f32[2,184,256]{2,1,0:T(8,128)S(1)}, u32[]{:S(2)}, u32[]{:S(2)}) collective-permute-start(f32[2,184,256]{2,1,0:T(8,128)} %get-tuple-element.24), channel_id=1, source_target_pairs={{4,0},{5,1},{6,2},{7,3},{8,4},{9,5},{10,6},{11,7},{12,8},{13,9},{1... | collective-permute-start | bytes 1130504 | tf_op jit(solution)/shard_map/ppermute | solution.py:536
  11.3 30.8 %collective-permute-start.3 = (f32[2,184,256]{2,1,0:T(8,128)}, f32[2,184,256]{2,1,0:T(8,128)S(1)}, u32[]{:S(2)}, u32[]{:S(2)}) collective-permute-start(f32[2,184,256]{2,1,0:T(8,128)} %get-tuple-element.25), channel_id=1, source_target_pairs={{0,4},{1,5},{2,6},{3,7},{4,8},{5,9},{6,10},{7,11},{8,12},{9,13},{1... | collective-permute-start | bytes 1130504 | tf_op jit(solution)/shard_map/ppermute | solution.py:536
  14.3 7.8 %collective-permute-start.4 = (f32[2,16,256]{2,1,0:T(8,128)}, f32[2,16,256]{2,1,0:T(8,128)S(1)}, u32[]{:S(2)}, u32[]{:S(2)}) collective-permute-start(f32[2,16,256]{2,1,0:T(8,128)} %get-tuple-element.26), channel_id=1, source_target_pairs={{4,3},{5,0},{6,1},{7,2},{8,7},{9,4},{10,5},{11,6},{12,11},{13,8},{... | collective-permute-start | bytes 98312 | tf_op jit(solution)/shard_map/ppermute | solution.py:536
  15.6 26.4 %collective-permute-start = (f32[2,64,256]{2,1,0:T(8,128)}, f32[2,64,256]{2,1,0:T(8,128)S(1)}, u32[]{:S(2)}, u32[]{:S(2)}) collective-permute-start(f32[2,64,256]{2,1,0:T(8,128)} %get-tuple-element.22), channel_id=1, source_target_pairs={{0,3},{1,0},{2,1},{3,2},{4,7},{5,4},{6,5},{7,6},{8,11},{9,8},{10,9... | collective-permute-start | bytes 393224 | tf_op jit(solution)/shard_map/ppermute | solution.py:536
  20.7 21.3 %collective-permute-start.1 = (f32[2,64,256]{2,1,0:T(8,128)}, f32[2,64,256]{2,1,0:T(8,128)S(1)}, u32[]{:S(2)}, u32[]{:S(2)}) collective-permute-start(f32[2,64,256]{2,1,0:T(8,128)} %get-tuple-element.23), channel_id=1, source_target_pairs={{0,1},{1,2},{2,3},{3,0},{4,5},{5,6},{6,7},{7,4},{8,9},{9,10},{10,1... | collective-permute-start | bytes 393224 | tf_op jit(solution)/shard_map/ppermute | solution.py:536
  22.1 10.4 %collective-permute-start.5 = (f32[2,16,256]{2,1,0:T(8,128)}, f32[2,16,256]{2,1,0:T(8,128)S(1)}, u32[]{:S(2)}, u32[]{:S(2)}) collective-permute-start(f32[2,16,256]{2,1,0:T(8,128)} %get-tuple-element.27), channel_id=1, source_target_pairs={{4,1},{5,2},{6,3},{7,0},{8,5},{9,6},{10,7},{11,4},{12,9},{13,10},{... | collective-permute-start | bytes 98312 | tf_op jit(solution)/shard_map/ppermute | solution.py:536
  32.5 6.4 %collective-permute-start.6 = (f32[2,16,256]{2,1,0:T(8,128)}, f32[2,16,256]{2,1,0:T(8,128)S(1)}, u32[]{:S(2)}, u32[]{:S(2)}) collective-permute-start(f32[2,16,256]{2,1,0:T(8,128)} %get-tuple-element.28), channel_id=1, source_target_pairs={{0,7},{1,4},{2,5},{3,6},{4,11},{5,8},{6,9},{7,10},{8,15},{9,12},{1... | collective-permute-start | bytes 98312 | tf_op jit(solution)/shard_map/ppermute | solution.py:536
  38.9 3.2 %collective-permute-start.7 = (f32[2,16,256]{2,1,0:T(8,128)}, f32[2,16,256]{2,1,0:T(8,128)S(1)}, u32[]{:S(2)}, u32[]{:S(2)}) collective-permute-start(f32[2,16,256]{2,1,0:T(8,128)} %get-tuple-element.29), channel_id=1, source_target_pairs={{0,5},{1,6},{2,7},{3,4},{4,9},{5,10},{6,11},{7,8},{8,13},{9,14},{1... | collective-permute-start | bytes 98312 | tf_op jit(solution)/shard_map/ppermute | solution.py:536
  52.5 6.6 %collective-permute-start.10 = (f32[8,128]{1,0:T(8,128)}, f32[8,128]{1,0:T(8,128)S(1)}, u32[]{:S(2)}, u32[]{:S(2)}) collective-permute-start(f32[8,128]{1,0:T(8,128)} %local_sums.1), channel_id=1, source_target_pairs={{0,3},{1,0},{2,1},{3,2},{4,7},{5,4},{6,5},{7,6},{8,11},{9,8},{10,9... | collective-permute-start | bytes 12296 | tf_op jit(solution)/shard_map/ppermute | solution.py:554
  54.5 5.9 %collective-permute-start.8 = (f32[8,128]{1,0:T(8,128)}, f32[8,128]{1,0:T(8,128)S(1)}, u32[]{:S(2)}, u32[]{:S(2)}) collective-permute-start(f32[8,128]{1,0:T(8,128)} %local_sums.1), channel_id=1, source_target_pairs={{0,1},{1,2},{2,3},{3,0},{4,5},{5,6},{6,7},{7,4},{8,9},{9,10},{10,1... | collective-permute-start | bytes 12296 | tf_op jit(solution)/shard_map/ppermute | solution.py:554
  54.6 6.4 %collective-permute-start.9 = (f32[8,128]{1,0:T(8,128)}, f32[8,128]{1,0:T(8,128)S(1)}, u32[]{:S(2)}, u32[]{:S(2)}) collective-permute-start(f32[8,128]{1,0:T(8,128)} %local_sums.1), channel_id=1, source_target_pairs={{0,2},{1,3},{2,0},{3,1},{4,6},{5,7},{6,4},{7,5},{8,10},{9,11},{10,... | collective-permute-start | bytes 12296 | tf_op jit(solution)/shard_map/ppermute | solution.py:554
  61.7 5.2 %collective-permute-start.11 = (f32[8,128]{1,0:T(8,128)S(1)}, f32[8,128]{1,0:T(8,128)S(1)}, u32[]{:S(2)}, u32[]{:S(2)}) collective-permute-start(f32[8,128]{1,0:T(8,128)S(1)} %add_add_fusion.1), channel_id=1, source_target_pairs={{0,4},{4,8},{8,12},{12,0},{1,5},{5,9},{9,13},{13,1},{2,6},{6,10},{... | collective-permute-start | bytes 12296 | tf_op jit(solution)/shard_map/ppermute | solution.py:554
  63.5 3.6 %collective-permute-start.12 = (f32[8,128]{1,0:T(8,128)S(1)}, f32[8,128]{1,0:T(8,128)S(1)}, u32[]{:S(2)}, u32[]{:S(2)}) collective-permute-start(f32[8,128]{1,0:T(8,128)S(1)} %add_add_fusion.1), channel_id=1, source_target_pairs={{0,8},{4,12},{8,0},{12,4},{1,9},{5,13},{9,1},{13,5},{2,10},{6,14},... | collective-permute-start | bytes 12296 | tf_op jit(solution)/shard_map/ppermute | solution.py:554
  65.4 2.8 %collective-permute-start.13 = (f32[8,128]{1,0:T(8,128)S(1)}, f32[8,128]{1,0:T(8,128)S(1)}, u32[]{:S(2)}, u32[]{:S(2)}) collective-permute-start(f32[8,128]{1,0:T(8,128)S(1)} %add_add_fusion.1), channel_id=1, source_target_pairs={{0,12},{4,0},{8,4},{12,8},{1,13},{5,1},{9,5},{13,9},{2,14},{6,2},{... | collective-permute-start | bytes 12296 | tf_op jit(solution)/shard_map/ppermute | solution.py:554
  84.3 47.3 %all-gather.7.cloned.1.call-start = ((), (), s32[]{:S(2)}) async-start(), calls=%async_computation.1 | async-start | bytes 1572864 | tf_op jit(solution)/shard_map/all_gather | solution.py:585
  85.0 70.1 %all-gather.9.cloned.1.call-start = ((), (), s32[]{:S(2)}) async-start(), calls=%async_computation.2 | async-start | bytes 1572864 | tf_op jit(solution)/shard_map/all_gather | solution.py:585
  85.7 92.6 %all-gather.11.cloned.1.call-start = ((), (), s32[]{:S(2)}) async-start(), calls=%async_computation.3 | async-start | bytes 1572864 | tf_op jit(solution)/shard_map/all_gather | solution.py:585
  88.4 13.2 %collective-permute-start.14 = (f32[64,128]{1,0:T(8,128)S(1)}, f32[64,128]{1,0:T(8,128)S(1)}, u32[]{:S(2)}, u32[]{:S(2)}) collective-permute-start(f32[64,128]{1,0:T(8,128)S(1)} %copy-done.9), channel_id=1, source_target_pairs={{0,1},{1,2},{2,3},{3,0},{4,5},{5,6},{6,7},{7,4},{8,9},{9,10},{10,1... | collective-permute-start | bytes 98312 | tf_op jit(solution)/shard_map/ppermute | solution.py:554
  88.5 13.1 %collective-permute-start.15 = (f32[64,128]{1,0:T(8,128)S(1)}, f32[64,128]{1,0:T(8,128)S(1)}, u32[]{:S(2)}, u32[]{:S(2)}) collective-permute-start(f32[64,128]{1,0:T(8,128)S(1)} %copy-done.9), channel_id=1, source_target_pairs={{0,2},{1,3},{2,0},{3,1},{4,6},{5,7},{6,4},{7,5},{8,10},{9,11},{10,... | collective-permute-start | bytes 98312 | tf_op jit(solution)/shard_map/ppermute | solution.py:554
  91.4 10.3 %collective-permute-start.16 = (f32[64,128]{1,0:T(8,128)S(1)}, f32[64,128]{1,0:T(8,128)S(1)}, u32[]{:S(2)}, u32[]{:S(2)}) collective-permute-start(f32[64,128]{1,0:T(8,128)S(1)} %copy-done.9), channel_id=1, source_target_pairs={{0,3},{1,0},{2,1},{3,2},{4,7},{5,4},{6,5},{7,6},{8,11},{9,8},{10,9... | collective-permute-start | bytes 98312 | tf_op jit(solution)/shard_map/ppermute | solution.py:554
  102.4 3.0 %collective-permute-start.17 = (f32[2]{0:T(128)S(1)}, f32[2]{0:T(128)S(1)}, u32[]{:S(2)}, u32[]{:S(2)}) collective-permute-start(f32[2]{0:T(128)S(1)} %broadcast_multiply_fusion.1), channel_id=1, source_target_pairs={{0,4},{4,8},{8,12},{12,0},{1,5},{5,9},{9,13},{13,1},{2,6},{6,10},{... | collective-permute-start | bytes 32 | tf_op jit(solution)/shard_map/ppermute | solution.py:554
  102.4 3.6 %collective-permute-start.18 = (f32[2]{0:T(128)S(1)}, f32[2]{0:T(128)S(1)}, u32[]{:S(2)}, u32[]{:S(2)}) collective-permute-start(f32[2]{0:T(128)S(1)} %broadcast_multiply_fusion.1), channel_id=1, source_target_pairs={{0,8},{4,12},{8,0},{12,4},{1,9},{5,13},{9,1},{13,5},{2,10},{6,14},... | collective-permute-start | bytes 32 | tf_op jit(solution)/shard_map/ppermute | solution.py:554
  103.4 2.7 %collective-permute-start.19 = (f32[2]{0:T(128)S(1)}, f32[2]{0:T(128)S(1)}, u32[]{:S(2)}, u32[]{:S(2)}) collective-permute-start(f32[2]{0:T(128)S(1)} %broadcast_multiply_fusion.1), channel_id=1, source_target_pairs={{0,12},{4,0},{8,4},{12,8},{1,13},{5,1},{9,5},{13,9},{2,14},{6,2},{... | collective-permute-start | bytes 32 | tf_op jit(solution)/shard_map/ppermute | solution.py:554
  (12 other events, 48.5 us)
Sparse Core Ops, SparseCore 0:
  84.4 24.3 all-gather.4
  110.9 20.6 all-gather.6
  133.7 21.2 all-gather.8
  157.0 21.2 all-gather.10

commit v2 on v1

--- a/solution.py
+++ b/solution.py
@@ -61,7 +61,7 @@
     return fields[5][...].astype(jnp.float32)
 
 
-def pack_kernel(levels, temp, salt, uvel, vvel, eta, mask, to_west, to_east, to_north, to_south, *corners):
+def pack_kernel(levels, temp, salt, uvel, vvel, eta, mask, to_west, to_east, to_north, to_south):
     members, _, rows, cols = temp.shape
     planes = 4 * levels + 2
     fields = (temp, salt, uvel, vvel, eta, mask)
@@ -85,10 +85,6 @@
             where = slice(group * LANE, (group + 1) * LANE)
             to_west[m, :, where] = west_parts[group]
             to_east[m, :, where] = east_parts[group]
-            corners[0][m, :, where] = west_parts[group][:CHUNK]
-            corners[1][m, :, where] = west_parts[group][rows - CHUNK :]
-            corners[2][m, :, where] = east_parts[group][:CHUNK]
-            corners[3][m, :, where] = east_parts[group][rows - CHUNK :]
 
 
 def whole(count):
@@ -102,12 +98,11 @@
     row_pack = -(-planes * WIDE // 8) * 8
     side = jax.ShapeDtypeStruct((members, rows, wide), jnp.float32)
     line = jax.ShapeDtypeStruct((members, row_pack, cols), jnp.float32)
-    corner = jax.ShapeDtypeStruct((members, CHUNK, wide), jnp.float32)
     return pl.pallas_call(
         functools.partial(pack_kernel, levels),
-        out_shape=(side, side, line, line, corner, corner, corner, corner),
+        out_shape=(side, side, line, line),
         in_specs=whole(6),
-        out_specs=tuple(whole(8)),
+        out_specs=tuple(whole(4)),
         compiler_params=pltpu.CompilerParams(vmem_limit_bytes=VMEM_LIMIT),
         name="pack_rims",
     )(temp, salt, uvel, vvel, eta, mask)
@@ -123,23 +118,23 @@
 
 
 def assemble(ext, fields, rims, m, levels):
-    from_east, from_west, from_north, from_south, ne, nw, se, sw = rims
+    from_east, from_west, from_north, from_south, north_sides, south_sides = rims
     planes = 4 * levels + 2
     rows, cols = fields[5].shape
-    bands = [(TOP - CHUNK, se, sw, 0, CHUNK)]
-    bands += [(TOP + a, from_east, from_west, a, CHUNK) for a in range(0, rows, CHUNK)]
-    bands += [(TOP + rows, ne, nw, 0, CHUNK)]
+    wide = groups_of(planes) * LANE
     for group in range(groups_of(planes)):
         where = slice(group * LANE, (group + 1) * LANE)
-        for at, east_ref, west_ref, start, size in bands:
-            east = east_ref[m, start : start + size, where]
-            west = west_ref[m, start : start + size, where]
-            slot = lanes_like(east.shape) // WIDE
-            odd = (slot & 1) == 1
+        where_west = slice(wide + group * LANE, wide + (group + 1) * LANE)
+        bands = [(TOP - CHUNK, south_sides[m, :, where], south_sides[m, :, where_west])]
+        for a in range(0, rows, CHUNK):
+            bands.append((TOP + a, from_east[m, a : a + CHUNK, where], from_west[m, a : a + CHUNK, where]))
+        bands.append((TOP + rows, north_sides[m, :, where], north_sides[m, :, where_west]))
+        for at, east, west in bands:
+            odd = ((lanes_like(east.shape) // WIDE) & 1) == 1
             joined = (jnp.where(odd, east, west), jnp.where(odd, west, east))
             for plane in range(group * PER_GROUP, min((group + 1) * PER_GROUP, planes)):
                 _, kind, offset = rim_place(plane)
-                ext[plane, at : at + size, cols : cols + LANE] = pltpu.roll(joined[kind], LANE - offset, 1)
+                ext[plane, at : at + CHUNK, cols : cols + LANE] = pltpu.roll(joined[kind], LANE - offset, 1)
     for plane in range(planes):
         ext[plane, TOP : TOP + rows, :cols] = load_plane(fields, m, plane, levels)
         ext[plane, TOP - WIDE : TOP, :cols] = from_south[m, plane * WIDE : (plane + 1) * WIDE, :]
@@ -275,7 +270,7 @@
 
 
 def sums_kernel(levels, total_rows, place, *refs):
-    fields, rims, out, scratch = refs[:6], refs[6:14], refs[14], refs[15:]
+    fields, rims, out, scratch = refs[:6], refs[6:12], refs[12], refs[13:]
     ext, planes, cor, inside, red = scratch
     members = fields[0].shape[0]
     rows, cols = fields[5].shape
@@ -338,7 +333,7 @@
     return pl.pallas_call(
         functools.partial(sums_kernel, levels, total_rows),
         out_shape=jax.ShapeDtypeStruct((8, LANE), jnp.float32),
-        in_specs=[pl.BlockSpec(memory_space=pltpu.SMEM)] + whole(14),
+        in_specs=[pl.BlockSpec(memory_space=pltpu.SMEM)] + whole(12),
         out_specs=pl.BlockSpec(memory_space=pltpu.VMEM),
         scratch_shapes=[
             pltpu.VMEM((4 * levels + 2,) + shape, jnp.float32),
@@ -348,6 +343,7 @@
             pltpu.VMEM((members, SUM_ROWS, LANE), jnp.float32),
         ],
         compiler_params=pltpu.CompilerParams(vmem_limit_bytes=VMEM_LIMIT),
+        cost_estimate=pl.CostEstimate(flops=10**8, bytes_accessed=4 * 10**6, transcendentals=0),
         name="local_sums",
     )(place, *fields, *rims)
 
@@ -409,191 +405,262 @@
 
 
 def advance_kernel(levels, total_rows, place, sums, *refs):
-    fields, rims = refs[:6], refs[6:14]
-    new_temp, new_salt, new_uvel, new_vvel, new_eta, zonal = refs[14:20]
-    ext, planes, after, cor, inside = refs[20:]
-    members = fields[0].shape[0]
+    fields, rims = refs[:6], refs[6:12]
+    out, zonal = refs[12:14]
+    ext, planes, after, cor, inside = refs[14:]
     rows, cols = fields[5].shape
     ocean_at = 4 * levels + 1
+    member = place[1]
     work = Planes(planes, RUN_NAMES)
     fill_rows(cor, inside, place[0], total_rows)
+    low, high = TOP - 8, TOP + rows + 8
+    assemble(ext, fields, rims, 0, levels)
+
+    def read(i):
+        return jnp.full((1, 1), sums[i % 8, member * SUM_LANES + i // 8], jnp.float32)
+
+    first, second = weights(read)
+    surface_start(ext, work, cor, inside, levels, rows)
+    powers(work, inside, "v0", "v1", "v2", low, high)
+    for a, b in chunks(low, high):
+        combine(work, first, ("v0", "v1", "v2"), "eta1", a, b)
+    surface_push(work, ext, levels, rows, "eta1", "pu", "pv", True)
+    surface_next(work, ext, cor, inside, levels, rows, "pu", "pv", "eta1", True, "w0")
+    powers(work, inside, "w0", "w1", "w2", low, high)
+    for a, b in chunks(low, high):
+        combine(work, second, ("w0", "w1", "w2"), "eta2", a, b)
+    for a, b in chunks(TOP, TOP + rows):
+        out[4 * levels, a - TOP : b - TOP, :] = work.get("eta2", a, b)[:, :cols]
+    for a, b in chunks(low, high):
+        ocean = ext[ocean_at, a:b, :]
+        for name, to_u, to_v in (("eta1", "pu", "pv"), ("eta2", "t2u", "t2v")):
+            _, east, west, north, south = work.sides(name, a, b)
+            work.put(to_u, a, b, GRAV * ocean * (east - west))
+            work.put(to_v, a, b, GRAV * ocean * (north - south))
+        cor[a:b, :] = STEP_DT * cor[a:b, :]
+    for a, b in chunks(TOP - CHUNK, TOP + rows + CHUNK):
+        work.put("p", a, b, jnp.zeros((b - a, cols + LANE), jnp.float32))
+        work.put("p2", a, b, jnp.zeros((b - a, cols + LANE), jnp.float32))
     zonal[...] = jnp.zeros_like(zonal)
-    low, high = TOP - 8, TOP + rows + 8
-
-    def one(m, carry):
-        assemble(ext, fields, rims, m, levels)
-
-        def read(i):
-            return jnp.full((1, 1), sums[i % 8, m * SUM_LANES + i // 8], jnp.float32)
-
-        first, second = weights(read)
-        surface_start(ext, work, cor, inside, levels, rows)
-        powers(work, inside, "v0", "v1", "v2", low, high)
-        for a, b in chunks(low, high):
-            combine(work, first, ("v0", "v1", "v2"), "eta1", a, b)
-        surface_push(work, ext, levels, rows, "eta1", "pu", "pv", True)
-        surface_next(work, ext, cor, inside, levels, rows, "pu", "pv", "eta1", True, "w0")
-        powers(work, inside, "w0", "w1", "w2", low, high)
-        for a, b in chunks(low, high):
-            combine(work, second, ("w0", "w1", "w2"), "eta2", a, b)
-        for a, b in chunks(TOP, TOP + rows):
-            new_eta[m, a - TOP : b - TOP, :] = work.get("eta2", a, b)[:, :cols]
-        for a, b in chunks(low, high):
-            ocean = ext[ocean_at, a:b, :]
-            for name, to_u, to_v in (("eta1", "pu", "pv"), ("eta2", "t2u", "t2v")):
-                _, east, west, north, south = work.sides(name, a, b)
-                work.put(to_u, a, b, GRAV * ocean * (east - west))
-                work.put(to_v, a, b, GRAV * ocean * (north - south))
-        for a, b in chunks(TOP - CHUNK, TOP + rows + CHUNK):
-            work.put("p", a, b, jnp.zeros((b - a, cols + LANE), jnp.float32))
-            work.put("p2", a, b, jnp.zeros((b - a, cols + LANE), jnp.float32))
-
-        def sides(ref, at, a, b):
-            here = ref[at, a:b, :]
-            east, west = east_west(here)
-            north, south = ref[at, a + 1 : b + 1, :], ref[at, a - 1 : b - 1, :]
-            return here, east - west, north - south, east + west + north + south - 4.0 * here
-
-        def step(ref, l, press, a, b):
-            ocean = ext[ocean_at, a:b, :]
-            temp, temp_x, temp_y, temp_l = sides(ref, l, a, b)
-            salt, salt_x, salt_y, salt_l = sides(ref, levels + l, a, b)
-            u, _, _, u_l = sides(ref, 2 * levels + l, a, b)
-            v, _, _, v_l = sides(ref, 3 * levels + l, a, b)
-            _, pe, pw, pn, ps = work.sides(press, a, b)
-            temp = ocean * (temp - ADV * (u * temp_x + v * temp_y) + KAPPA * temp_l)
-            salt = ocean * (salt - ADV * (u * salt_x + v * salt_y) + KAPPA * salt_l)
-            u, v = momentum(ocean, cor[a:b, :], u, v, pe - pw, pn - ps, u_l, v_l)
-            return temp, salt, u, v
-
-        def add_press(ref, l, press, a, b):
-            dens = BETA_S * ref[levels + l, a:b, :] - ALPHA_T * ref[l, a:b, :]
-            work.put(press, a, b, work.get(press, a, b) + PRESS_K * dens)
-
-        def level(l, carry):
-            for a, b in chunks(TOP - CHUNK, TOP + rows + CHUNK):
-                add_press(ext, l, "p", a, b)
-            for a, b in chunks(low, high):
-                temp, salt, u, v = step(ext, l, "p", a, b)
-                after[l, a:b, :] = temp
-                after[levels + l, a:b, :] = salt
-                after[2 * levels + l, a:b, :] = u - work.get("pu", a, b)
-                after[3 * levels + l, a:b, :] = v - work.get("pv", a, b)
-            for a, b in chunks(low, high):
-                add_press(after, l, "p2", a, b)
-            for a, b in chunks(TOP, TOP + rows):
-                temp, salt, u, v = step(after, l, "p2", a, b)
-                u = u - work.get("t2u", a, b)
-                v = v - work.get("t2v", a, b)
-                here = slice(a - TOP, b - TOP)
-                new_temp[m, l, here, :] = temp[:, :cols]
-                new_salt[m, l, here, :] = salt[:, :cols]
-                new_uvel[m, l, here, :] = u[:, :cols]
-                new_vvel[m, l, here, :] = v[:, :cols]
-                total = jnp.sum(v[:, :cols], axis=1, keepdims=True)
-                lane = lanes_like((b - a, LANE))
-                zonal[here, :] = jnp.where(lane == m * levels + l, total, zonal[here, :])
-            return carry
-
-        lax.fori_loop(0, levels, level, 0)
+
+    def step(ref, l, press, a, b, width):
+        def sides(value, above, below):
+            east, west = east_west(value)
+            east, west = east[:, :width], west[:, :width]
+            north, south = above[:, :width], below[:, :width]
+            return value[:, :width], east, west, north, south
+
+        def of(at):
+            return sides(ref[at, a:b, :], ref[at, a + 1 : b + 1, :], ref[at, a - 1 : b - 1, :])
+
+        ocean = ext[ocean_at, a:b, :width]
+        coriolis = cor[a:b, :width]
+        u, east, west, north, south = of(2 * levels + l)
+        around_u = (east + west) + (north + south)
+        v, east, west, north, south = of(3 * levels + l)
+        around_v = (east + west) + (north + south)
+        _, pe, pw, pn, ps = sides(work.get(press, a, b), work.get(press, a + 1, b + 1), work.get(press, a - 1, b - 1))
+        keep = 1.0 - STEP_DT * DRAG_K - 4.0 * VISCOSITY
+        new_u = ocean * ((keep * u + VISCOSITY * around_u) + (coriolis * v - (pe - pw)))
+        new_v = ocean * ((keep * v + VISCOSITY * around_v) - (coriolis * u + (pn - ps)))
+        flow_u, flow_v = ADV * u, ADV * v
+        results = []
+        for at in (l, levels + l):
+            here, east, west, north, south = of(at)
+            carried = flow_u * (east - west) + flow_v * (north - south)
+            spread = (1.0 - 4.0 * KAPPA) * here + KAPPA * ((east + west) + (north + south))
+            results.append(ocean * (spread - carried))
+        return results[0], results[1], new_u, new_v
+
+    def add_press(ref, l, press, a, b):
+        factor = PRESS_K * 0.5 * STEP_DT
+        dens = (factor * BETA_S) * ref[levels + l, a:b, :] - (factor * ALPHA_T) * ref[l, a:b, :]
+        work.put(press, a, b, work.get(press, a, b) + dens)
+
+    def level(l, carry):
+        for a in range(TOP - CHUNK, TOP + rows + CHUNK, 8):
+            add_press(ext, l, "p", a, a + 8)
+        for a in range(low, high, 8):
+            temp, salt, u, v = step(ext, l, "p", a, a + 8, cols + LANE)
+            after[l, a : a + 8, :] = temp
+            after[levels + l, a : a + 8, :] = salt
+            after[2 * levels + l, a : a + 8, :] = u - work.get("pu", a, a + 8)
+            after[3 * levels + l, a : a + 8, :] = v - work.get("pv", a, a + 8)
+        for a in range(low, high, 8):
+            add_press(after, l, "p2", a, a + 8)
+        for a in range(TOP, TOP + rows, 8):
+            temp, salt, u, v = step(after, l, "p2", a, a + 8, cols)
+            here = slice(a - TOP, a - TOP + 8)
+            v = v - work.get("t2v", a, a + 8)[:, :cols]
+            out[l, here, :] = temp
+            out[levels + l, here, :] = salt
+            out[2 * levels + l, here, :] = u - work.get("t2u", a, a + 8)[:, :cols]
+            out[3 * levels + l, here, :] = v
+            total = jnp.sum(v, axis=1, keepdims=True)
+            lane = lanes_like((8, LANE))
+            zonal[here, :] = jnp.where(lane == member * levels + l, total, zonal[here, :])
         return carry
 
-    lax.fori_loop(0, members, one, 0)
+    lax.fori_loop(0, levels, level, 0)
 
 
 def advance(place, sums, fields, rims, total_rows):
     members, levels, rows, cols = fields[0].shape
     shape = plane_shape(rows, cols)
-    volume = jax.ShapeDtypeStruct((members, levels, rows, cols), jnp.float32)
-    surface = jax.ShapeDtypeStruct((members, rows, cols), jnp.float32)
+
+    def of_member(value):
+        rest = value.shape[1:]
+        return pl.BlockSpec((1,) + rest, lambda i, place: (place[1],) + (0,) * len(rest))
+
+    def fixed(dims):
+        return pl.BlockSpec(dims, lambda i, place: (0,) * len(dims))
+
+    mask_spec = fixed(fields[5].shape)
+    final = (4 * levels + 1, rows, cols)
     return pl.pallas_call(
         functools.partial(advance_kernel, levels, total_rows),
-        out_shape=(volume,) * 4 + (surface, jax.ShapeDtypeStruct((rows, LANE), jnp.float32)),
-        in_specs=[pl.BlockSpec(memory_space=pltpu.SMEM)] * 2 + whole(14),
-        out_specs=tuple(whole(6)),
-        scratch_shapes=[
-            pltpu.VMEM((4 * levels + 2,) + shape, jnp.float32),
-            pltpu.VMEM((len(RUN_NAMES),) + shape, jnp.float32),
-            pltpu.VMEM((4 * levels,) + shape, jnp.float32),
-            pltpu.VMEM(shape, jnp.float32),
-            pltpu.VMEM(shape, jnp.float32),
-        ],
+        out_shape=(jax.ShapeDtypeStruct(final, jnp.float32), jax.ShapeDtypeStruct((rows, LANE), jnp.float32)),
+        grid_spec=pltpu.PrefetchScalarGridSpec(
+            num_scalar_prefetch=1,
+            grid=(1,),
+            in_specs=[pl.BlockSpec(memory_space=pltpu.SMEM)]
+            + [of_member(value) for value in fields[:5]]
+            + [mask_spec]
+            + [of_member(value) for value in rims],
+            out_specs=(fixed(final), fixed((rows, LANE))),
+            scratch_shapes=[
+                pltpu.VMEM((4 * levels + 2,) + shape, jnp.float32),
+                pltpu.VMEM((len(RUN_NAMES),) + shape, jnp.float32),
+                pltpu.VMEM((4 * levels,) + shape, jnp.float32),
+                pltpu.VMEM(shape, jnp.float32),
+                pltpu.VMEM(shape, jnp.float32),
+            ],
+        ),
         compiler_params=pltpu.CompilerParams(vmem_limit_bytes=VMEM_LIMIT),
+        cost_estimate=pl.CostEstimate(flops=10**8, bytes_accessed=4 * 10**6, transcendentals=0),
         name="advance",
     )(place, sums, *fields, *rims)
 
 
+def pick_kernel(levels, choice, *refs):
+    count = len(refs) - 6
+    sources, outs, sem = refs[:count], refs[count : count + 5], refs[count + 5]
+    slots = outs[0].shape[0]
+
+    def parts(s, source):
+        for f in range(4):
+            yield source.at[pl.ds(f * levels, levels)], outs[f].at[s]
+        yield source.at[4 * levels], outs[4].at[s]
+
+    for s in range(slots):
+        for k in range(count):
+
+            @pl.when(choice[s] == k)
+            def _():
+                for i, (source, target) in enumerate(parts(s, sources[k])):
+                    pltpu.make_async_copy(source, target, sem.at[s, i]).start()
+
+    for s in range(slots):
+        for i, (source, target) in enumerate(parts(s, sources[0])):
+            pltpu.make_async_copy(source, target, sem.at[s, i]).wait()
+
+
+def pick(choice, sources, slots, levels):
+    _, rows, cols = sources[0].shape
+    volume = jax.ShapeDtypeStruct((slots, levels, rows, cols), jnp.float32)
+    surface = jax.ShapeDtypeStruct((slots, rows, cols), jnp.float32)
+    return pl.pallas_call(
+        functools.partial(pick_kernel, levels),
+        out_shape=(volume,) * 4 + (surface,),
+        in_specs=[pl.BlockSpec(memory_space=pltpu.SMEM)] + [pl.BlockSpec(memory_space=pl.ANY)] * len(sources),
+        out_specs=(pl.BlockSpec(memory_space=pl.ANY),) * 5,
+        scratch_shapes=[pltpu.SemaphoreType.DMA((slots, 5))],
+        name="pick",
+    )(choice, *sources)
+
+
+def shift(value, axis, by, wrap):
+    count = lax.axis_size(axis)
+    pairs = [(i, (i + by) % count) for i in range(count) if wrap or 0 <= i + by < count]
+    return lax.ppermute(value, axis, pairs)
+
+
 def exchange_rims(packed):
-    to_west, to_east, to_north, to_south, west_low, west_high, east_low, east_high = packed
-    count_y, count_x = lax.axis_size("gridy"), lax.axis_size("gridx")
-
-    def move(value, north, east):
-        pairs = []
-        for j in range(count_y):
-            for i in range(count_x):
-                if 0 <= j + north < count_y:
-                    pairs.append((j * count_x + i, (j + north) * count_x + (i + east) % count_x))
-        return lax.ppermute(value, ("gridy", "gridx"), pairs)
-
-    return (
-        move(to_west, 0, -1),
-        move(to_east, 0, 1),
-        move(to_south, -1, 0),
-        move(to_north, 1, 0),
-        move(west_low, -1, -1),
-        move(east_low, -1, 1),
-        move(west_high, 1, -1),
-        move(east_high, 1, 1),
-    )
+    to_west, to_east, to_north, to_south = packed
+    rows = to_west.shape[1]
+    from_east, from_west = shift(to_west, "gridx", -1, True), shift(to_east, "gridx", 1, True)
+    from_north, from_south = shift(to_south, "gridy", -1, False), shift(to_north, "gridy", 1, False)
+    low = jnp.concatenate([from_east[:, :CHUNK], from_west[:, :CHUNK]], axis=2)
+    high = jnp.concatenate([from_east[:, rows - CHUNK :], from_west[:, rows - CHUNK :]], axis=2)
+    north_sides, south_sides = shift(low, "gridy", -1, False), shift(high, "gridy", 1, False)
+    return from_east, from_west, from_north, from_south, north_sides, south_sides
 
 
 def total_over(value, axis):
     count = lax.axis_size(axis)
-    if count <= 4:
-        moved = [
-            lax.ppermute(value, axis, [(i, (i + shift) % count) for i in range(count)]) for shift in range(1, count)
-        ]
-        for part in moved:
-            value = value + part
-        return value
+    if count & (count - 1):
+        return lax.psum(value, axis)
     step = 1
     while step < count:
-        if count % (2 * step):
-            return lax.psum(value, axis)
         value = value + lax.ppermute(value, axis, [(i, i ^ step) for i in range(count)])
         step *= 2
     return value
 
 
-def swap_members(value):
-    return lax.all_gather(value, "member", axis=0, tiled=True)
+def swap(value):
+    return lax.ppermute(value, "member", [(0, 1), (1, 0)])
+
+
+def first_and_both(wanted, side, members):
+    away = wanted // members != side
+    index = wanted - (1 - side) * members
+    takes = [jnp.any(away & (index == m)) for m in range(members)]
+    return jnp.where(takes[0], 0, 1).astype(jnp.int32), takes[0] & takes[1]
 
 
 def shards(temp, salt, uvel, vvel, eta, land_mask, clone_source):
     members, levels, rows, cols = temp.shape
-    tile_row = lax.axis_index("gridy")
+    assert members == 2 and lax.axis_size("member") == 2
+    tile_row, side = lax.axis_index("gridy"), lax.axis_index("member")
     total_rows = rows * lax.axis_size("gridy")
     total_cols = cols * lax.axis_size("gridx")
-    place = (tile_row * rows).astype(jnp.int32).reshape(1)
+    their_source = swap(clone_source)
+    here_first, here_both = first_and_both(clone_source, side, members)
+    sent_first, sent_both = first_and_both(their_source, 1 - side, members)
+
+    first_row = (tile_row * rows).astype(jnp.int32)
     fields = (temp, salt, uvel, vvel, eta, land_mask)
     rims = exchange_rims(pack_rims(*fields))
-    sums = local_sums(place, fields, rims, total_rows)
+    sums = local_sums(first_row.reshape(1), fields, rims, total_rows)
     sums = total_over(total_over(sums, "gridx"), "gridy")
-    *state, zonal = advance(place, sums, fields, rims, total_rows)
-    side = lax.axis_index("member")
-    count = lax.axis_size("member")
-    every = [lax.all_gather(value, "member", axis=0, tiled=True) for value in state]
-    picked = [jnp.take(value, clone_source, axis=0) for value in every]
-
-    zonal_whole = total_over(zonal, "gridx")[:, : members * levels].reshape(rows, members, levels)
+
+    sent, sent_zonal = advance(jnp.stack([first_row, sent_first]), sums, fields, rims, total_rows)
+    arrived = swap(sent)
+    other, other_zonal = advance(jnp.stack([first_row, 1 - sent_first]), sums, fields, rims, total_rows)
+
+    zonal_whole = total_over(sent_zonal + other_zonal, "gridx")[:, : members * levels].reshape(rows, members, levels)
     zonal_whole = jnp.transpose(zonal_whole, (1, 2, 0))
     zonal_scale = 1.0 / jnp.sqrt(jnp.float32(total_cols))
     score_scale = 1.0 / jnp.sqrt(jnp.float32(levels * total_rows))
     latitude = (tile_row * rows + jnp.arange(rows, dtype=jnp.int32)).astype(jnp.float32) + 0.5
     overturn = jnp.cumsum(zonal_whole, axis=1) * zonal_scale
     score = total_over(jnp.sum(overturn * (latitude / total_rows), axis=(1, 2)) * score_scale, "gridy")
-    every_score = lax.all_gather(score, "member", axis=0, tiled=True)
+    their_score = swap(score)
+    every_score = jnp.where(side == 0, jnp.concatenate([score, their_score]), jnp.concatenate([their_score, score]))
     clone_weight = jnp.take(every_score, clone_source, axis=0) - jnp.mean(every_score)
+
+    away = clone_source // members != side
+    index = clone_source % members
+    choice = jnp.where(away, jnp.where(index == here_first, 2, 3), jnp.where(index == sent_first, 0, 1))
+    choice = choice.astype(jnp.int32)
+
+    def with_second():
+        return pick(choice, (sent, other, arrived, swap(other)), members, levels)
+
+    def without_second():
+        return pick(choice, (sent, other, arrived), members, levels)
+
+    picked = lax.cond(here_both | sent_both, with_second, without_second)
     return (*picked, overturn, clone_weight)
 
 

time: 189 us -> 103 us (0.54)
  waiting for transfers between devices: 78.2 us -> 29.5 us
  blocking collectives: 14.2 us -> 0 us
  between operations: 15.3 us -> 5.21 us
  local copies, waits for them, and re-layouts: 11.2 us -> 1.56 us
  starting transfers between devices: 36.1 us -> 27.6 us
  Pallas kernels: 27.7 us -> 32.6 us
    all_gather x4 -> x0, waiting for transfers between devices: 58.1 us -> none  [shards(): lax.all_gather(value, 'member', axis=0, tiled=True)]
    ppermute x20 -> x17, waiting for transfers between devices: 18.7 us -> 29.5 us  [the longest x3 15.7 us: swap(): return lax.ppermute(value, 'member', [(0, 1), (1, 0)])]
    all_gather x1 -> x0, blocking collectives: 9.3 us -> none  [shards(): lax.all_gather(value, 'member', axis=0, tiled=True)]
    ppermute x20 -> x17, starting transfers between devices: 35.9 us -> 27.6 us  [the longest x6 13.7 us: shift(): return lax.ppermute(value, axis, pairs)]
    gather x5 -> x0, local copies, waits for them, and re-layouts: 7.78 us -> none  [shards(): picked = [jnp.take(value, clone_source, axis=0) for value in every]]
    unnamed x1 -> x0, blocking collectives: 4.94 us -> none
    pallas_call x1 -> x2, Pallas kernels: 15.4 us -> 18.3 us  [advance(): pl.pallas_call(functools.partial(advance_kernel, levels, total_rows), out...]
    select_n x3 -> x1, other arithmetic: 2.21 us -> 0.01 us  [shards(): jnp.take(every_score, clone_source, axis=0) - jnp.mean(every_score)]
  transfers between devices with their start and end apart: 24 -> 17, of which waited for: 14 -> 9; matrix products, arithmetic and copies ran while one was open for 5% -> 5% of each run, Pallas kernels for 0% -> 9%
where the time goes in v2:
time: 103 us; the launch traced here: 102 us
  Pallas kernels  32.6 us (32%)
  waiting for transfers between devices  29.5 us (29%)
  starting transfers between devices  27.6 us (27%)
  other arithmetic  5.94 us (6%)
  between operations  5.21 us (5%)
  local copies, waits for them, and re-layouts  1.56 us (2%)
    pallas_call x2, Pallas kernels, advance(): pl.pallas_call(functools.partial(advance_kernel, levels, total_rows), out...  18.3 us
    ppermute x3, waiting for transfers between devices, swap(): return lax.ppermute(value, 'member', [(0, 1), (1, 0)])  15.7 us
    ppermute x6, starting transfers between devices, shift(): return lax.ppermute(value, axis, pairs)  13.7 us
    ppermute x8, waiting for transfers between devices, total_over(): lax.ppermute(value, axis, [(i, i ^ step) for i in range(count)])  11.2 us
    pallas_call x1, Pallas kernels, local_sums(): pl.pallas_call(functools.partial(sums_kernel, levels, total_rows), out_sh...  9.52 us
    ppermute x8, starting transfers between devices, total_over(): lax.ppermute(value, axis, [(i, i ^ step) for i in range(count)])  9.19 us
    ppermute x3, starting transfers between devices, swap(): return lax.ppermute(value, 'member', [(0, 1), (1, 0)])  4.69 us
    pallas_call x1, Pallas kernels, pack_rims(): pl.pallas_call(functools.partial(pack_kernel, levels), out_shape=(side, s...  2.75 us
  transfers between devices with their start and end apart: 17, of which 9 were waited for; matrix products, arithmetic and copies ran while one was open for 5% of the time, Pallas kernels for 9%

profile of v2, /device:TPU:0, one launch (start us, length us, event | category | flops | bytes accessed | tf_op | source)
XLA Modules:
  0.0 102.4 jit_solution(2459887669367037542)
XLA Ops:
  0.6 2.7 %pack_rims.1 = (f32[2,64,256]{2,1,0:T(8,128)}, f32[2,64,256]{2,1,0:T(8,128)}, f32[2,184,256]{2,1,0:T(8,128)}, f32[2,184,256]{2,1,0:T(8,128)}) custom-call(f32[2,4,64,256]{3,2,1,0:T(8,128)} %refs_0_.5, f32[2,4,64,256]{3,2,1,0:T(8,128)} %refs_1_.5, f32[2,4,64,256]{3,2,1,0:T(8,128)} %refs_2_.5, f32[2,4,64,256]{3,2,1,0:T(8,128)} %refs_3_.5, ...), custom_call_target="tpu_custom_call" | custom-call | tf_op jit(solution)/shard_map/pack_rims/pallas_call | solution.py:101
  3.4 5.0 %collective-permute-start.2 = (f32[2,64,256]{2,1,0:T(8,128)}, f32[2,64,256]{2,1,0:T(8,128)S(1)}, u32[]{:S(2)}, u32[]{:S(2)}) collective-permute-start(f32[2,64,256]{2,1,0:T(8,128)} %get-tuple-element.44), channel_id=1, source_target_pairs={{0,3},{1,0},{2,1},{3,2},{4,7},{5,4},{6,5},{7,6},{8,11},{9,8},{10,9... | collective-permute-start | bytes 393224 | tf_op jit(solution)/shard_map/ppermute | solution.py:585
  8.4 1.3 %collective-permute-start.4 = (f32[2,184,256]{2,1,0:T(8,128)}, f32[2,184,256]{2,1,0:T(8,128)S(1)}, u32[]{:S(2)}, u32[]{:S(2)}) collective-permute-start(f32[2,184,256]{2,1,0:T(8,128)} %get-tuple-element.46), channel_id=1, source_target_pairs={{4,0},{8,4},{12,8},{5,1},{9,5},{13,9},{6,2},{10,6},{14,10},{7,3},{... | collective-permute-start | bytes 1130504 | tf_op jit(solution)/shard_map/ppermute | solution.py:585
  9.7 3.1 %collective-permute-start.5 = (f32[2,184,256]{2,1,0:T(8,128)}, f32[2,184,256]{2,1,0:T(8,128)S(1)}, u32[]{:S(2)}, u32[]{:S(2)}) collective-permute-start(f32[2,184,256]{2,1,0:T(8,128)} %get-tuple-element.47), channel_id=1, source_target_pairs={{0,4},{4,8},{8,12},{1,5},{5,9},{9,13},{2,6},{6,10},{10,14},{3,7},{... | collective-permute-start | bytes 1130504 | tf_op jit(solution)/shard_map/ppermute | solution.py:585
  12.8 2.6 %collective-permute-done.3.refs_7_ = f32[2,64,256]{2,1,0:T(8,128)S(1)} collective-permute-done((f32[2,64,256]{2,1,0:T(8,128)}, f32[2,64,256]{2,1,0:T(8,128)S(1)}, u32[]{:S(2)}, u32[]{:S(2)}) %collective-permute-start.3) | collective-permute-done | bytes 131104 | tf_op jit(solution)/shard_map/ppermute | solution.py:585
  15.4 1.3 %collective-permute-start.6 = (f32[2,16,512]{2,1,0:T(8,128)S(1)}, f32[2,16,512]{2,1,0:T(8,128)S(1)}, u32[]{:S(2)}, u32[]{:S(2)}) collective-permute-start(f32[2,16,512]{2,1,0:T(8,128)S(1)} %pad_maximum_fusion), channel_id=1, source_target_pairs={{4,0},{8,4},{12,8},{5,1},{9,5},{13,9},{6,2},{10,6},{14,10},{7,3},{... | collective-permute-start | bytes 196616 | tf_op jit(solution)/shard_map/ppermute | solution.py:585
  16.8 3.0 %collective-permute-start.7 = (f32[2,16,512]{2,1,0:T(8,128)S(1)}, f32[2,16,512]{2,1,0:T(8,128)S(1)}, u32[]{:S(2)}, u32[]{:S(2)}) collective-permute-start(f32[2,16,512]{2,1,0:T(8,128)S(1)} %pad_maximum_fusion.1), channel_id=1, source_target_pairs={{0,4},{4,8},{8,12},{1,5},{5,9},{9,13},{2,6},{6,10},{10,14},{3,7},{... | collective-permute-start | bytes 196616 | tf_op jit(solution)/shard_map/ppermute | solution.py:585
  19.8 1.6 %collective-permute-start.1 = (s32[2]{0:T(128)S(1)}, s32[2]{0:T(128)S(1)}, u32[]{:S(2)}, u32[]{:S(2)}) collective-permute-start(s32[2]{0:T(128)S(1)} %copy-done.8), channel_id=1, source_target_pairs={{0,16},{16,0},{1,17},{17,1},{2,18},{18,2},{3,19},{19,3},{4,20},{20... | collective-permute-start | bytes 32 | tf_op jit(solution)/shard_map/ppermute | solution.py:611
  22.3 9.5 %local_sums.1 = f32[8,128]{1,0:T(8,128)} custom-call(s32[1]{0:T(128)} %bitcast.place, f32[2,4,64,256]{3,2,1,0:T(8,128)} %refs_0_.5, f32[2,4,64,256]{3,2,1,0:T(8,128)} %refs_1_.5, f32[2,4,64,256]{3,2,1,0:T(8,128)} %refs_2_.5, f32[2,4,64,256]{3,2,1,0:T(8,128)} %refs_3_.5, f32[2,64,256]{2,1,0:T(8,128)} %refs_4_.5, s32[64,256]{1,0:T(8,128)} %refs_5_.5, ...), custom_call_target="tpu_custom_call" | custom-call | flops 100000000 | bytes 4000000 | tf_op jit(solution)/shard_map/local_sums/pallas_call | solution.py:333
  31.8 1.3 %collective-permute-start.8 = (f32[8,128]{1,0:T(8,128)}, f32[8,128]{1,0:T(8,128)S(1)}, u32[]{:S(2)}, u32[]{:S(2)}) collective-permute-start(f32[8,128]{1,0:T(8,128)} %local_sums.1), channel_id=1, source_target_pairs={{0,1},{1,0},{2,3},{3,2},{4,5},{5,4},{6,7},{7,6},{8,9},{9,8},{10,11... | collective-permute-start | bytes 12296 | tf_op jit(solution)/shard_map/ppermute | solution.py:605
  33.8 1.8 %collective-permute-done.8 = f32[8,128]{1,0:T(8,128)S(1)} collective-permute-done((f32[8,128]{1,0:T(8,128)}, f32[8,128]{1,0:T(8,128)S(1)}, u32[]{:S(2)}, u32[]{:S(2)}) %collective-permute-start.8) | collective-permute-done | bytes 4128 | tf_op jit(solution)/shard_map/ppermute | solution.py:605
  38.5 2.3 %collective-permute-done.9 = f32[8,128]{1,0:T(8,128)S(1)} collective-permute-done((f32[8,128]{1,0:T(8,128)S(1)}, f32[8,128]{1,0:T(8,128)S(1)}, u32[]{:S(2)}, u32[]{:S(2)}) %collective-permute-start.9) | collective-permute-done | bytes 4128 | tf_op jit(solution)/shard_map/ppermute | solution.py:605
  42.2 3.1 %collective-permute-start.11 = (f32[8,128]{1,0:T(8,128)S(1)}, f32[8,128]{1,0:T(8,128)S(1)}, u32[]{:S(2)}, u32[]{:S(2)}) collective-permute-start(f32[8,128]{1,0:T(8,128)S(1)} %add.62), channel_id=1, source_target_pairs={{0,8},{4,12},{8,0},{12,4},{1,9},{5,13},{9,1},{13,5},{2,10},{6,14},... | collective-permute-start | bytes 12296 | tf_op jit(solution)/shard_map/ppermute | solution.py:605
  47.5 9.1 %advance.3 = (f32[17,64,256]{2,1,0:T(8,128)S(1)}, f32[64,128]{1,0:T(8,128)}) custom-call(s32[2]{0:T(128)} %get-tuple-element.73.place, f32[8,128]{1,0:T(8,128)} %add.63.sums, f32[2,4,64,256]{3,2,1,0:T(8,128)} %refs_0_.5, f32[2,4,64,256]{3,2,1,0:T(8,128)} %refs_1_.5, f32[2,4,64,256]{3,2,1,0:T(8,128)} %refs_2_.5, f32[2,4,64,256]{3,2,1,0:T(8,128)} %refs_3_.5, ...), custom_call_target="tpu_custom_call" | custom-call | flops 100000000 | bytes 4000000 | tf_op jit(solution)/shard_map/advance/pallas_call | solution.py:520
  56.6 9.2 %advance.2 = (f32[17,64,256]{2,1,0:T(8,128)S(1)}, f32[64,128]{1,0:T(8,128)}) custom-call(s32[2]{0:T(128)} %get-tuple-element.72.place, f32[8,128]{1,0:T(8,128)} %add.63.sums, f32[2,4,64,256]{3,2,1,0:T(8,128)} %refs_0_.5, f32[2,4,64,256]{3,2,1,0:T(8,128)} %refs_1_.5, f32[2,4,64,256]{3,2,1,0:T(8,128)} %refs_2_.5, f32[2,4,64,256]{3,2,1,0:T(8,128)} %refs_3_.5, ...), custom_call_target="tpu_custom_call" | custom-call | flops 100000000 | bytes 4000000 | tf_op jit(solution)/shard_map/advance/pallas_call | solution.py:520
  66.6 1.3 %collective-permute-start.13 = (f32[64,128]{1,0:T(8,128)S(1)}, f32[64,128]{1,0:T(8,128)S(1)}, u32[]{:S(2)}, u32[]{:S(2)}) collective-permute-start(f32[64,128]{1,0:T(8,128)S(1)} %add.64), channel_id=1, source_target_pairs={{0,1},{1,0},{2,3},{3,2},{4,5},{5,4},{6,7},{7,6},{8,9},{9,8},{10,11... | collective-permute-start | bytes 98312 | tf_op jit(solution)/shard_map/ppermute | solution.py:605
  67.9 2.6 %collective-permute-done.13 = f32[64,128]{1,0:T(8,128)S(1)} collective-permute-done((f32[64,128]{1,0:T(8,128)S(1)}, f32[64,128]{1,0:T(8,128)S(1)}, u32[]{:S(2)}, u32[]{:S(2)}) %collective-permute-start.13) | collective-permute-done | bytes 32800 | tf_op jit(solution)/shard_map/ppermute | solution.py:605
  72.8 1.6 %collective-permute-start.12 = (f32[17,64,256]{2,1,0:T(8,128)S(1)}, f32[17,64,256]{2,1,0:T(8,128)S(1)}, u32[]{:S(2)}, u32[]{:S(2)}) collective-permute-start(f32[17,64,256]{2,1,0:T(8,128)S(1)} %get-tuple-element.48), channel_id=1, source_target_pairs={{0,16},{16,0},{1,17},{17,1},{2,18},{18,2},{3,19},{19,3},{4,20},{20... | collective-permute-start | bytes 3342344 | tf_op jit(solution)/shard_map/ppermute | solution.py:611
  77.2 2.0 %collective-permute-start.16 = (f32[2]{0:T(128)S(1)}, f32[2]{0:T(128)S(1)}, u32[]{:S(2)}, u32[]{:S(2)}) collective-permute-start(f32[2]{0:T(128)S(1)} %fusion.3), channel_id=1, source_target_pairs={{0,8},{4,12},{8,0},{12,4},{1,9},{5,13},{9,1},{13,5},{2,10},{6,14},... | collective-permute-start | bytes 32 | tf_op jit(solution)/shard_map/ppermute | solution.py:605
  79.2 1.5 %collective-permute-done.16 = f32[2]{0:T(128)S(1)} collective-permute-done((f32[2]{0:T(128)S(1)}, f32[2]{0:T(128)S(1)}, u32[]{:S(2)}, u32[]{:S(2)}) %collective-permute-start.16) | collective-permute-done | bytes 40 | tf_op jit(solution)/shard_map/ppermute | solution.py:605
  80.7 1.5 %collective-permute-start.17 = (f32[2]{0:T(128)S(1)}, f32[2]{0:T(128)S(1)}, u32[]{:S(2)}, u32[]{:S(2)}) collective-permute-start(f32[2]{0:T(128)S(1)} %add.73), channel_id=1, source_target_pairs={{0,16},{16,0},{1,17},{17,1},{2,18},{18,2},{3,19},{19,3},{4,20},{20... | collective-permute-start | bytes 32 | tf_op jit(solution)/shard_map/ppermute | solution.py:611
  82.2 15.7 %collective-permute-done.17 = f32[2]{0:T(128)S(1)} collective-permute-done((f32[2]{0:T(128)S(1)}, f32[2]{0:T(128)S(1)}, u32[]{:S(2)}, u32[]{:S(2)}) %collective-permute-start.17) | collective-permute-done | bytes 40 | tf_op jit(solution)/shard_map/ppermute | solution.py:611
  100.4 2.0 %conditional.1 = ((f32[2,4,64,256]{3,2,1,0:T(8,128)}, f32[2,4,64,256]{3,2,1,0:T(8,128)}, f32[2,4,64,256]{3,2,1,0:T(8,128)}, f32[2,4,64,256]{3,2,1,0:T(8,128)}, f32[2,64,256]{2,1,0:T(8,128)})) conditional(s32[]{:T(128)} %convert_element_type.10, (s32[2]{0:T(128)S(1)}, f32[17,64,256]{2,1,0:T(8,128)S(1)}, f32[17,64,256]{2,1,0:T(8,128)S(1)}, ...), branch_computations={%region_4.5_spmd, %region_5.6_spmd} | conditional | bytes 8912972 | solution.py:663
  100.4 2.0 %pick.2 = (f32[2,4,64,256]{3,2,1,0:T(8,128)}, f32[2,4,64,256]{3,2,1,0:T(8,128)}, f32[2,4,64,256]{3,2,1,0:T(8,128)}, f32[2,4,64,256]{3,2,1,0:T(8,128)}, f32[2,64,256]{2,1,0:T(8,128)}) custom-call(s32[2]{0:T(128)S(1)} %get-tuple-element.16.choice, f32[17,64,256]{2,1,0:T(8,128)S(1)} %get-tuple-element.17.refs_0_, f32[17,64,256]{2,1,0:T(8,128)S(1)} %get-tuple-element.18.refs_1_, ...), custom_call_target="tpu_custom_call" | custom-call | tf_op jit(solution)/shard_map/cond/branch_0_fun/pick/pallas_call | solution.py:572
  (58 shorter events, 11.9 us)
Async XLA Ops:
  0.6 19.2 %copy-start.8 = (s32[2]{0:T(128)S(1)}, s32[2]{0:T(128)}, u32[]{:S(2)}) copy-start(s32[2]{0:T(128)} %param.15) | copy-start | bytes 28
  3.4 9.4 %collective-permute-start.2 = (f32[2,64,256]{2,1,0:T(8,128)}, f32[2,64,256]{2,1,0:T(8,128)S(1)}, u32[]{:S(2)}, u32[]{:S(2)}) collective-permute-start(f32[2,64,256]{2,1,0:T(8,128)} %get-tuple-element.44), channel_id=1, source_target_pairs={{0,3},{1,0},{2,1},{3,2},{4,7},{5,4},{6,5},{7,6},{8,11},{9,8},{10,9... | collective-permute-start | bytes 393224 | tf_op jit(solution)/shard_map/ppermute | solution.py:585
  8.4 7.0 %collective-permute-start.3 = (f32[2,64,256]{2,1,0:T(8,128)}, f32[2,64,256]{2,1,0:T(8,128)S(1)}, u32[]{:S(2)}, u32[]{:S(2)}) collective-permute-start(f32[2,64,256]{2,1,0:T(8,128)} %get-tuple-element.45), channel_id=1, source_target_pairs={{0,1},{1,2},{2,3},{3,0},{4,5},{5,6},{6,7},{7,4},{8,9},{9,10},{10,1... | collective-permute-start | bytes 393224 | tf_op jit(solution)/shard_map/ppermute | solution.py:585
  8.4 13.0 %collective-permute-start.4 = (f32[2,184,256]{2,1,0:T(8,128)}, f32[2,184,256]{2,1,0:T(8,128)S(1)}, u32[]{:S(2)}, u32[]{:S(2)}) collective-permute-start(f32[2,184,256]{2,1,0:T(8,128)} %get-tuple-element.46), channel_id=1, source_target_pairs={{4,0},{8,4},{12,8},{5,1},{9,5},{13,9},{6,2},{10,6},{14,10},{7,3},{... | collective-permute-start | bytes 1130504 | tf_op jit(solution)/shard_map/ppermute | solution.py:585
  9.7 11.7 %collective-permute-start.5 = (f32[2,184,256]{2,1,0:T(8,128)}, f32[2,184,256]{2,1,0:T(8,128)S(1)}, u32[]{:S(2)}, u32[]{:S(2)}) collective-permute-start(f32[2,184,256]{2,1,0:T(8,128)} %get-tuple-element.47), channel_id=1, source_target_pairs={{0,4},{4,8},{8,12},{1,5},{5,9},{9,13},{2,6},{6,10},{10,14},{3,7},{... | collective-permute-start | bytes 1130504 | tf_op jit(solution)/shard_map/ppermute | solution.py:585
  12.8 8.7 %copy-start.2 = (f32[2,64,256]{2,1,0:T(8,128)}, f32[2,64,256]{2,1,0:T(8,128)S(1)}, u32[]{:S(2)}) copy-start(f32[2,64,256]{2,1,0:T(8,128)S(1)} %collective-permute-done.2.refs_6_) | copy-start | bytes 393220
  15.4 6.1 %copy-start.3 = (f32[2,64,256]{2,1,0:T(8,128)}, f32[2,64,256]{2,1,0:T(8,128)S(1)}, u32[]{:S(2)}) copy-start(f32[2,64,256]{2,1,0:T(8,128)S(1)} %collective-permute-done.3.refs_7_) | copy-start | bytes 393220
  15.4 6.0 %collective-permute-start.6 = (f32[2,16,512]{2,1,0:T(8,128)S(1)}, f32[2,16,512]{2,1,0:T(8,128)S(1)}, u32[]{:S(2)}, u32[]{:S(2)}) collective-permute-start(f32[2,16,512]{2,1,0:T(8,128)S(1)} %pad_maximum_fusion), channel_id=1, source_target_pairs={{4,0},{8,4},{12,8},{5,1},{9,5},{13,9},{6,2},{10,6},{14,10},{7,3},{... | collective-permute-start | bytes 196616 | tf_op jit(solution)/shard_map/ppermute | solution.py:585
  16.8 4.6 %collective-permute-start.7 = (f32[2,16,512]{2,1,0:T(8,128)S(1)}, f32[2,16,512]{2,1,0:T(8,128)S(1)}, u32[]{:S(2)}, u32[]{:S(2)}) collective-permute-start(f32[2,16,512]{2,1,0:T(8,128)S(1)} %pad_maximum_fusion.1), channel_id=1, source_target_pairs={{0,4},{4,8},{8,12},{1,5},{5,9},{9,13},{2,6},{6,10},{10,14},{3,7},{... | collective-permute-start | bytes 196616 | tf_op jit(solution)/shard_map/ppermute | solution.py:585
  19.8 21.0 %collective-permute-start.1 = (s32[2]{0:T(128)S(1)}, s32[2]{0:T(128)S(1)}, u32[]{:S(2)}, u32[]{:S(2)}) collective-permute-start(s32[2]{0:T(128)S(1)} %copy-done.8), channel_id=1, source_target_pairs={{0,16},{16,0},{1,17},{17,1},{2,18},{18,2},{3,19},{19,3},{4,20},{20... | collective-permute-start | bytes 32 | tf_op jit(solution)/shard_map/ppermute | solution.py:611
  21.4 0.6 copy-start.6
  21.4 0.8 copy-start
  21.4 0.9 copy-start.1
  31.8 3.8 %collective-permute-start.8 = (f32[8,128]{1,0:T(8,128)}, f32[8,128]{1,0:T(8,128)S(1)}, u32[]{:S(2)}, u32[]{:S(2)}) collective-permute-start(f32[8,128]{1,0:T(8,128)} %local_sums.1), channel_id=1, source_target_pairs={{0,1},{1,0},{2,3},{3,2},{4,5},{5,4},{6,7},{7,6},{8,9},{9,8},{10,11... | collective-permute-start | bytes 12296 | tf_op jit(solution)/shard_map/ppermute | solution.py:605
  36.3 4.5 %collective-permute-start.9 = (f32[8,128]{1,0:T(8,128)S(1)}, f32[8,128]{1,0:T(8,128)S(1)}, u32[]{:S(2)}, u32[]{:S(2)}) collective-permute-start(f32[8,128]{1,0:T(8,128)S(1)} %add.60), channel_id=1, source_target_pairs={{0,2},{1,3},{2,0},{3,1},{4,6},{5,7},{6,4},{7,5},{8,10},{9,11},{10,... | collective-permute-start | bytes 12296 | tf_op jit(solution)/shard_map/ppermute | solution.py:605
  40.8 1.3 %collective-permute-start.10 = (f32[8,128]{1,0:T(8,128)S(1)}, f32[8,128]{1,0:T(8,128)S(1)}, u32[]{:S(2)}, u32[]{:S(2)}) collective-permute-start(f32[8,128]{1,0:T(8,128)S(1)} %add.61), channel_id=1, source_target_pairs={{0,4},{4,0},{8,12},{12,8},{1,5},{5,1},{9,13},{13,9},{2,6},{6,2},{1... | collective-permute-start | bytes 12296 | tf_op jit(solution)/shard_map/ppermute | solution.py:605
  42.2 4.7 %collective-permute-start.11 = (f32[8,128]{1,0:T(8,128)S(1)}, f32[8,128]{1,0:T(8,128)S(1)}, u32[]{:S(2)}, u32[]{:S(2)}) collective-permute-start(f32[8,128]{1,0:T(8,128)S(1)} %add.62), channel_id=1, source_target_pairs={{0,8},{4,12},{8,0},{12,4},{1,9},{5,13},{9,1},{13,5},{2,10},{6,14},... | collective-permute-start | bytes 12296 | tf_op jit(solution)/shard_map/ppermute | solution.py:605
  56.6 9.2 %copy-start.7 = (f32[64,128]{1,0:T(8,128)S(1)}, f32[64,128]{1,0:T(8,128)}, u32[]{:S(2)}) copy-start(f32[64,128]{1,0:T(8,128)} %get-tuple-element.56) | copy-start | bytes 98308
  66.6 3.9 %collective-permute-start.13 = (f32[64,128]{1,0:T(8,128)S(1)}, f32[64,128]{1,0:T(8,128)S(1)}, u32[]{:S(2)}, u32[]{:S(2)}) collective-permute-start(f32[64,128]{1,0:T(8,128)S(1)} %add.64), channel_id=1, source_target_pairs={{0,1},{1,0},{2,3},{3,2},{4,5},{5,4},{6,7},{7,6},{8,9},{9,8},{10,11... | collective-permute-start | bytes 98312 | tf_op jit(solution)/shard_map/ppermute | solution.py:605
  70.5 4.8 %collective-permute-start.14 = (f32[64,128]{1,0:T(8,128)S(1)}, f32[64,128]{1,0:T(8,128)S(1)}, u32[]{:S(2)}, u32[]{:S(2)}) collective-permute-start(f32[64,128]{1,0:T(8,128)S(1)} %add.65), channel_id=1, source_target_pairs={{0,2},{1,3},{2,0},{3,1},{4,6},{5,7},{6,4},{7,5},{8,10},{9,11},{10,... | collective-permute-start | bytes 98312 | tf_op jit(solution)/shard_map/ppermute | solution.py:605
  72.8 27.6 %collective-permute-start.12 = (f32[17,64,256]{2,1,0:T(8,128)S(1)}, f32[17,64,256]{2,1,0:T(8,128)S(1)}, u32[]{:S(2)}, u32[]{:S(2)}) collective-permute-start(f32[17,64,256]{2,1,0:T(8,128)S(1)} %get-tuple-element.48), channel_id=1, source_target_pairs={{0,16},{16,0},{1,17},{17,1},{2,18},{18,2},{3,19},{19,3},{4,20},{20... | collective-permute-start | bytes 3342344 | tf_op jit(solution)/shard_map/ppermute | solution.py:611
  76.0 1.1 %collective-permute-start.15 = (f32[2]{0:T(128)S(1)}, f32[2]{0:T(128)S(1)}, u32[]{:S(2)}, u32[]{:S(2)}) collective-permute-start(f32[2]{0:T(128)S(1)} %broadcast_multiply_fusion.1), channel_id=1, source_target_pairs={{0,4},{4,0},{8,12},{12,8},{1,5},{5,1},{9,13},{13,9},{2,6},{6,2},{1... | collective-permute-start | bytes 32 | tf_op jit(solution)/shard_map/ppermute | solution.py:605
  77.2 3.5 %collective-permute-start.16 = (f32[2]{0:T(128)S(1)}, f32[2]{0:T(128)S(1)}, u32[]{:S(2)}, u32[]{:S(2)}) collective-permute-start(f32[2]{0:T(128)S(1)} %fusion.3), channel_id=1, source_target_pairs={{0,8},{4,12},{8,0},{12,4},{1,9},{5,13},{9,1},{13,5},{2,10},{6,14},... | collective-permute-start | bytes 32 | tf_op jit(solution)/shard_map/ppermute | solution.py:605
  80.7 17.2 %collective-permute-start.17 = (f32[2]{0:T(128)S(1)}, f32[2]{0:T(128)S(1)}, u32[]{:S(2)}, u32[]{:S(2)}) collective-permute-start(f32[2]{0:T(128)S(1)} %add.73), channel_id=1, source_target_pairs={{0,16},{16,0},{1,17},{17,1},{2,18},{18,2},{3,19},{19,3},{4,20},{20... | collective-permute-start | bytes 32 | tf_op jit(solution)/shard_map/ppermute | solution.py:611
  (1 other events, 0.6 us)
